TPU v7x, 128 devices: a whole 4x4x4 slice. The times are simulated.
128 devices in a mesh: img: 16 (over z, y), txt: 8 (over x, core).
Axes of the slice: x: 4, y: 4, z: 4, core: 2. Of those that a mesh axis runs over, the one named last changes fastest.
Arguments:
- image_emb: float32 [16384, 1280], P(('img', 'txt')), may hold values from -8 to 8
- text_emb: float32 [16384, 1280], P(('txt', 'img')), may hold values from -8 to 8
- logit_scale: float32 [], replicated, may hold values from 8 to 12
Outputs:
- loss: float32 [], replicated
- image_grad: float32 [16384, 1280], P(('img', 'txt'))
- text_grad: float32 [16384, 1280], P(('txt', 'img'))
All inputs are finite; a program needn't handle non-finite values.
Results may differ from a plain program's by a relative error of at most 0.0003.
Values sent between devices are 32-bit elements; how exact they have to be, the bound alone decides.
A program may use at most 128 MiB of HBM per device.

v0:
```python
import jax
import jax.numpy as jnp
from jax import lax
from jax.sharding import PartitionSpec as P


def on_device(image_emb, text_emb, logit_scale):
    own_rows = image_emb.shape[0]
    txt_count = lax.axis_size("txt")
    img_count = lax.axis_size("img")
    img_rows = lax.all_gather(image_emb, "txt", axis=0, tiled=True)
    txt_cols = lax.all_gather(text_emb, "img", axis=0, tiled=True)
    logits = logit_scale * lax.dot_general(
        img_rows,
        txt_cols,
        (((1,), (1,)), ((), ())),
        precision=lax.Precision.HIGHEST,
        preferred_element_type=jnp.float32,
    )
    row_peak = lax.pmax(jnp.max(logits, axis=1), "txt")
    col_peak = lax.pmax(jnp.max(logits, axis=0), "img")
    row_total = lax.psum(jnp.sum(jnp.exp(logits - row_peak[:, None]), axis=1), "txt")
    col_total = lax.psum(jnp.sum(jnp.exp(logits - col_peak[None, :]), axis=0), "img")
    row_lse = row_peak + jnp.log(row_total)
    col_lse = col_peak + jnp.log(col_total)
    rows_global = lax.axis_index("img") * img_rows.shape[0] + jnp.arange(
        img_rows.shape[0], dtype=jnp.int32
    )
    cols_global = lax.axis_index("txt") * txt_cols.shape[0] + jnp.arange(
        txt_cols.shape[0], dtype=jnp.int32
    )
    diagonal_mask = (rows_global[:, None] == cols_global[None, :]).astype(jnp.float32)
    diagonal_sum = jnp.sum(logits * diagonal_mask)
    local_part = jnp.sum(row_lse) / txt_count + jnp.sum(col_lse) / img_count - 2.0 * diagonal_sum
    summed_loss = lax.psum(local_part, ("img", "txt"))
    loss = summed_loss / (2.0 * own_rows * txt_count * img_count)
    logit_grad = (
        0.5 * (jnp.exp(logits - row_lse[:, None]) + jnp.exp(logits - col_lse[None, :]))
        - diagonal_mask
    )
    image_part = logit_scale * jnp.dot(
        logit_grad, txt_cols, precision=lax.Precision.HIGHEST, preferred_element_type=jnp.float32
    )
    text_part = logit_scale * lax.dot_general(
        logit_grad,
        img_rows,
        (((0,), (0,)), ((), ())),
        precision=lax.Precision.HIGHEST,
        preferred_element_type=jnp.float32,
    )
    image_whole = lax.psum(image_part, "txt")
    text_whole = lax.psum(text_part, "img")
    image_grad = lax.dynamic_slice_in_dim(
        image_whole, lax.axis_index("txt") * own_rows, own_rows, 0
    )
    text_grad = lax.dynamic_slice_in_dim(text_whole, lax.axis_index("img") * own_rows, own_rows, 0)
    return (loss, image_grad, text_grad)


def solution(mesh):
    in_specs = (P(("img", "txt"), None), P(("txt", "img"), None), P())
    out_specs = (P(), P(("img", "txt"), None), P(("txt", "img"), None))
    return jax.shard_map(
        on_device, mesh=mesh, in_specs=in_specs, out_specs=out_specs, check_vma=False
    )
```

profile of v0, /device:TPU:1, one launch (start us, length us, event | category | flops | bytes accessed | tf_op | source)
XLA Modules:
  0.0 580.9 jit_solution(6795951442946973709)
XLA Ops:
  7.2 0.0 all-gather.3.cloned.1.call-start
  7.2 0.7 all-gather.3.cloned.1.call-update
  7.9 0.0 all-gather.5.cloned.1.call-start
  7.9 0.7 all-gather.5.cloned.1.call-update
  8.6 0.0 all-reduce.3.cloned.1.call-start
  9.4 40.4 %all-gather.3.cloned.1.call-done = f32[1024,1280]{1,0:T(8,128)} async-done(((f32[128,1280]{1,0:T(8,128)}), f32[1024,1280]{1,0:T(8,128)}) %all-gather.3.cloned.1.call-update) | async-done | bytes 5242896 | tf_op jit(solution)/shard_map/all_gather | solution.py:11
  49.8 82.3 %all-gather.5.cloned.1.call-done = f32[2048,1280]{1,0:T(8,128)} async-done(((f32[128,1280]{1,0:T(8,128)}), f32[2048,1280]{1,0:T(8,128)}) %all-gather.5.cloned.1.call-update) | async-done | bytes 10485776 | tf_op jit(solution)/shard_map/all_gather | solution.py:12
  132.1 45.1 %multiply_reduce_fusion.1 = (f32[1024]{0:T(1024)S(1)}, f32[1024,2048]{1,0:T(8,128)}) fusion(f32[]{:T(128)S(6)} %copy.8, f32[1024,1280]{1,0:T(8,128)} %all-gather.3.cloned.1.call-done, f32[2048,1280]{1,0:T(8,128)} %all-gather.5.cloned.1.call-done), kind=kOutput, calls=%fused_computation.8 | convolution fusion | flops 32216449024 | bytes 24121348 | tf_op jit(solution)/shard_map/dot_general | solution.py:13
  177.2 12.4 %pmax.14 = f32[1024]{0:T(1024)S(1)} all-reduce(f32[1024]{0:T(1024)S(1)} %get-tuple-element.10), channel_id=1, replica_groups=mesh['img'=16,'txt'=8] {'txt'}, use_global_device_ids=true, to_apply=%region_1.0 | all-reduce | flops 1024 | bytes 8192 | tf_op jit(solution)/shard_map/pmax | solution.py:20
  189.6 7.0 %fusion = (f32[]{:T(128)}, f32[1024]{0:T(1024)S(1)}, f32[2048]{0:T(1024)S(1)}) fusion(f32[1024,2048]{1,0:T(8,128)} %get-tuple-element.11, s32[2048]{0:T(1024)S(1)} %iota_add_fusion, f32[]{:T(128)S(6)} %copy.8, s32[1024]{0:T(1024)S(1)} %iota_add_fusion.1, f32[1024]{0:T(1024)S(1)} %pmax.14), kind=kLoop, calls=%fused_computation.3 | loop fusion | flops 14676991 | bytes 8417288 | tf_op jit(solution)/shard_map/reduce_sum | solution.py:33
  196.6 14.5 %psum.35 = f32[1024]{0:T(1024)S(1)} all-reduce(f32[1024]{0:T(1024)S(1)} %get-tuple-element.4), channel_id=1, replica_groups=mesh['img'=16,'txt'=8] {'txt'}, use_global_device_ids=true, to_apply=%region_3.0 | all-reduce | flops 1024 | bytes 8192 | tf_op jit(solution)/shard_map/psum | solution.py:22
  211.1 0.6 fusion.5
  211.7 32.0 %pmax.15 = f32[2048]{0:T(1024)S(1)} all-reduce(f32[2048]{0:T(1024)S(1)} %get-tuple-element.5), channel_id=1, replica_groups=mesh['img'=16,'txt'=8] {'img'}, use_global_device_ids=true, to_apply=%region_6.0 | all-reduce | flops 2048 | bytes 16384 | tf_op jit(solution)/shard_map/pmax | solution.py:21
  243.7 4.8 exponential_reduce_fusion
  248.5 29.2 %psum.36 = f32[2048]{0:T(1024)S(1)} all-reduce(f32[2048]{0:T(1024)S(1)} %exponential_reduce_fusion), channel_id=1, replica_groups=mesh['img'=16,'txt'=8] {'img'}, use_global_device_ids=true, to_apply=%region_8.0 | all-reduce | flops 2048 | bytes 16384 | tf_op jit(solution)/shard_map/psum | solution.py:23
  277.7 0.6 fusion.4
  278.3 42.8 %convolution_multiply_fusion.1 = f32[1024,1280]{1,0:T(8,128)} fusion(f32[2048,1280]{1,0:T(8,128)} %all-gather.5.cloned.1.call-done, f32[]{:T(128)S(6)} %copy.8, f32[1024,2048]{1,0:T(8,128)} %get-tuple-element.11, f32[2048]{0:T(1024)S(1)} %get-tuple-element.7, f32[1024]{0:T(1024)S(1)} %get-tuple-element.9, s32[2048]{0:T(1024)S(1)} %iota_add_fusion, ...), kind=kOutput, calls=%fused_computation.9 | convolution fusion | flops 32230342656 | bytes 24141828 | tf_op jit(solution)/shard_map/dot_general | solution.py:41
  321.1 0.3 all-reduce.5.cloned.1.call-start
  321.4 41.0 %convolution_multiply_fusion = f32[2048,1280]{1,0:T(8,128)} fusion(f32[1024,1280]{1,0:T(8,128)} %all-gather.3.cloned.1.call-done, f32[]{:T(128)S(6)} %copy.8, f32[1024,2048]{1,0:T(8,128)} %get-tuple-element.11, f32[2048]{0:T(1024)S(1)} %get-tuple-element.7, f32[1024]{0:T(1024)S(1)} %get-tuple-element.9, s32[2048]{0:T(1024)S(1)} %iota_add_fusion, ...), kind=kOutput, calls=%fused_computation.2 | convolution fusion | flops 32231653376 | bytes 24141828 | tf_op jit(solution)/shard_map/dot_general | solution.py:44
  364.3 77.9 %psum.37 = f32[]{:T(128)} all-reduce(f32[]{:T(128)S(6)} %sub.42), channel_id=1, replica_groups=mesh['img'=16,'txt'=8] {'img','txt'}, use_global_device_ids=true, to_apply=%region_11.0 | all-reduce | flops 1 | bytes 8 | tf_op jit(solution)/shard_map/psum | solution.py:35
  442.8 0.0 all-reduce.3.cloned.1.call-done
  442.9 2.0 constant_dynamic-slice_fusion.1
  444.8 126.4 %all-reduce.5.cloned.1.call-done = f32[2048,1280]{1,0:T(8,128)} async-done(((f32[2048,1280]{1,0:T(8,128)}), f32[2048,1280]{1,0:T(8,128)}) %all-reduce.5.cloned.1.call-update) | async-done | bytes 10485776 | tf_op jit(solution)/shard_map/psum | solution.py:52
  571.2 2.0 constant_dynamic-slice_fusion
  (4 shorter events, 0.0 us)
Async XLA Ops:
  7.2 42.7 %all-gather.3.cloned.1.call-start = ((), (), s32[]{:S(2)}) async-start(), calls=%async_computation | async-start | bytes 5898240 | tf_op jit(solution)/shard_map/all_gather | solution.py:11
  7.9 124.2 %all-gather.5.cloned.1.call-start = ((), (), s32[]{:S(2)}) async-start(), calls=%async_computation.1 | async-start | bytes 11141120 | tf_op jit(solution)/shard_map/all_gather | solution.py:12
  8.6 434.2 %all-reduce.3.cloned.1.call-start = ((), (), s32[]{:S(2)}) async-start(), calls=%async_computation.2 | async-start | bytes 10485760 | tf_op jit(solution)/shard_map/psum | solution.py:51
  321.1 250.1 %all-reduce.5.cloned.1.call-start = ((), (), s32[]{:S(2)}) async-start(), calls=%async_computation.3 | async-start | bytes 20971520 | tf_op jit(solution)/shard_map/psum | solution.py:52
Sparse Core Ops, SparseCore 0:
  9.7 40.0 all-gather.2
  52.0 80.1 all-gather.4
  321.2 85.9 all-reduce.2
  410.7 160.4 all-reduce.4
where the time goes:
time: 581 us
  waiting for transfers between devices  251 us (43%)
  blocking collectives  166 us (29%)
  matrix products  129 us (22%)
  between operations  18.2 us (3%)
  other arithmetic  13 us (2%)
    psum x1, waiting for transfers between devices, on_device(): text_whole = lax.psum(text_part, 'img')  126 us
    all_gather x1, waiting for transfers between devices, on_device(): txt_cols = lax.all_gather(text_emb, 'img', axis=0, tiled=True)  82.3 us
    psum x1, blocking collectives, on_device(): summed_loss = lax.psum(local_part, ('img', 'txt'))  77.9 us
    dot_general x1, matrix products, on_device(): lax.dot_general(img_rows, txt_cols, (((1,), (1,)), ((), ())), precision=l...  45.1 us
    dot_general x1, matrix products, on_device(): jnp.dot(logit_grad, txt_cols, precision=lax.Precision.HIGHEST, preferred_...  42.8 us
    dot_general x1, matrix products, on_device(): lax.dot_general(logit_grad, img_rows, (((0,), (0,)), ((), ())), precision...  41 us
    all_gather x1, waiting for transfers between devices, on_device(): img_rows = lax.all_gather(image_emb, 'txt', axis=0, tiled=True)  40.4 us
    pmax x1, blocking collectives, on_device(): col_peak = lax.pmax(jnp.max(logits, axis=0), 'img')  32 us
  transfers between devices with their start and end apart: 4, of which 3 were waited for; matrix products, arithmetic and copies ran while one was open for 7% of the time, Pallas kernels for 0%

commit v1 on v0

v1 whole, which is shorter than its diff:
```python
import functools

import jax
import jax.numpy as jnp
from jax import lax
from jax.experimental import pallas as pl
from jax.experimental.pallas import tpu as pltpu
from jax.sharding import PartitionSpec as P

MESH = pl.DeviceIdType.MESH
BF16, F32 = jnp.bfloat16, jnp.float32
LOG2E = 1.4426950408889634
LN2 = 0.6931471805599453

STEP = (0, 1, 3, 2)
ROWS = 128
HALF = ROWS // 2
E = 1280
IMG, TXT = 1024, 2048


def step_of(q):
    return q + q // 2 - 2 * (q // 3)


def dot(a, b, ca, cb):
    return lax.dot_general(a, b, (((ca,), (cb,)), ((), ())), preferred_element_type=F32)


def dot3(ah, al, bh, bl, ca, cb):
    return dot(ah, bh, ca, cb) + (dot(ah, bl, ca, cb) + dot(al, bh, ca, cb))


class Wires:
    def __init__(self, send_sem, recv_sem):
        self.send_sem, self.recv_sem = send_sem, recv_sem
        self.sent, self.n_recv, self.arrivals = [], 0, {}

    def open(self, key, ref, *index):
        self.arrivals[key] = (ref, index, self.n_recv)
        self.n_recv += 1

    def send(self, src, key, dev):
        dst, index, n = self.arrivals[key]
        dst = dst.at[index]
        s = len(self.sent)
        cp = pltpu.make_async_remote_copy(
            src_ref=src,
            dst_ref=dst,
            send_sem=self.send_sem.at[s],
            recv_sem=self.recv_sem.at[n],
            device_id=dev,
            device_id_type=MESH,
        )
        cp.start()
        self.sent.append(dst.shape)

    def wait(self, key):
        dst, index, n = self.arrivals.pop(key)
        dst = dst.at[index]
        pltpu.make_async_copy(dst, dst, self.recv_sem.at[n]).wait()
        return dst

    def flush(self, like):
        for s, shape in enumerate(self.sent):
            ref = like(shape)
            pltpu.make_async_copy(ref, ref, self.send_sem.at[s]).wait()
        self.sent = []


def merge(parts):
    top = functools.reduce(jnp.maximum, [m for m, _ in parts])
    total = sum(s * jnp.exp2(m - top) for m, s in parts)
    return top, total


def kernel(
    scale_ref, img_ref, txt_ref,
    loss_ref, img_out, txt_out,
    Ib, Tb, Ih, Il, Th, Tl, L, Ph, Pl,
    row_m, row_s, rst, cst, acc, lbuf,
    tland, iland, eye,
    send_sem, recv_sem, local_sem,
):
    i, t = lax.axis_index("img"), lax.axis_index("txt")
    x, k = t // 2, t % 2
    z, y = i // 4, i % 4

    def dev(dx=0, dy=0, dz=0, dk=0):
        return (((z + dz) % 4) * 4 + (y + dy) % 4, ((x + dx) % 4) * 2 + (k + dk) % 2)

    sib = dev(dk=1)
    xs = {1: dev(dx=1), -1: dev(dx=3), 2: dev(dx=2)}
    ys = {1: dev(dy=1), -1: dev(dy=3), 2: dev(dy=2)}
    zs = {1: dev(dz=1), -1: dev(dz=3), 2: dev(dz=2)}
    peers = [sib, *xs.values(), *ys.values(), *zs.values()]
    barrier = pltpu.get_barrier_semaphore()
    for peer in peers:
        pl.semaphore_signal(barrier, inc=1, device_id=peer, device_id_type=MESH)
    pl.semaphore_wait(barrier, len(peers))

    w = Wires(send_sem, recv_sem)

    def like(shape):
        if shape[-1] == E:
            return Ib.at[0, pl.ds(0, shape[0])]
        return {2: lbuf, 3: rst if shape[-2] == 8 else cst}[len(shape)].at[0]
    lo, hi = pl.ds(0, HALF), pl.ds(HALF, HALF)

    def T(qz, qy, part):
        return Tb.at[qz * 4 + qy, part]

    for qz in range(4):
        for qy in range(4):
            for name, part, split in (("A", lo, qz == 0 and qy == 3), ("B", hi, qz == 3 and qy == 0)):
                if (qz, qy) == (0, 0):
                    continue
                if split:
                    at = 0 if name == "A" else HALF
                    w.open((name, qz, qy, 0), Tb, qz * 4 + qy, pl.ds(at, 32))
                    w.open((name, qz, qy, 1), Tb, qz * 4 + qy, pl.ds(at + 32, 32))
                else:
                    w.open((name, qz, qy), Tb, qz * 4 + qy, part)
    for q in (1, 2):
        w.open(("I", q), Ib, 2 * q)
    w.open(("I", 3, 0), Ib, 6, lo)
    w.open(("I", 3, 1), Ib, 6, hi)
    for q in range(4):
        w.open(("S", q), Ib, 2 * q + 1)

    own_t = pltpu.make_async_copy(txt_ref, Tb.at[0], local_sem.at[0])
    own_i = pltpu.make_async_copy(img_ref, Ib.at[0], local_sem.at[1])
    w.send(txt_ref.at[lo], ("A", 0, 2), ys[1])
    w.send(txt_ref.at[lo], ("A", 0, 1), ys[-1])
    w.send(txt_ref.at[hi], ("B", 2, 0), zs[1])
    w.send(txt_ref.at[hi], ("B", 1, 0), zs[-1])
    w.send(img_ref, ("I", 2), xs[1])
    w.send(img_ref, ("I", 1), xs[-1])
    w.send(txt_ref.at[lo], ("A", 2, 0), zs[1])
    w.send(txt_ref.at[lo], ("A", 1, 0), zs[-1])
    w.send(txt_ref.at[hi], ("B", 0, 2), ys[1])
    w.send(txt_ref.at[hi], ("B", 0, 1), ys[-1])
    w.send(img_ref, ("S", 0), sib)
    own_t.start()
    own_i.start()

    for q, back in ((2, 1), (1, -1)):
        part = 0 if q == 2 else 1
        src = w.wait(("A", 0, q))
        w.send(T(0, q, pl.ds(32 * part, 32)), ("A", 0, 3, part), ys[back])
        w.send(src, ("A", 2, q), zs[1])
        w.send(src, ("A", 1, q), zs[-1])
        src = w.wait(("B", q, 0))
        w.send(T(q, 0, pl.ds(HALF + 32 * part, 32)), ("B", 3, 0, part), zs[back])
        w.send(src, ("B", q, 2), ys[1])
        w.send(src, ("B", q, 1), ys[-1])
    for q, back in ((2, 1), (1, -1)):
        src = w.wait(("I", q))
        part = 0 if q == 2 else 1
        w.send(Ib.at[2 * q, pl.ds(HALF * part, HALF)], ("I", 3, part), xs[back])
        w.send(src, ("S", q), sib)
    for name, where, a, b in (("A", (0, 3), 2, 1), ("B", (3, 0), 2, 1)):
        w.wait((name, *where, 0))
        w.wait((name, *where, 1))
        if name == "A":
            w.send(T(0, 3, lo), ("A", 2, 3), zs[1])
            w.send(T(0, 3, lo), ("A", 1, 3), zs[-1])
        else:
            w.send(T(3, 0, hi), ("B", 3, 2), ys[1])
            w.send(T(3, 0, hi), ("B", 3, 1), ys[-1])

    def second_ring(q):
        if q in (0, 3):
            w.send(w.wait(("A", 2, q)), ("A", 3, q), zs[1])
            w.send(w.wait(("B", q, 2)), ("B", q, 3), ys[1])
        else:
            w.send(w.wait(("A", 1, q)), ("A", 3, q), zs[-1])
            w.send(w.wait(("B", q, 1)), ("B", q, 3), ys[-1])

    second_ring(0)
    own_i.wait()
    own_t.wait()
    rows_iota = lax.broadcasted_iota(jnp.int32, (ROWS, ROWS), 0)
    cols_iota = lax.broadcasted_iota(jnp.int32, (ROWS, ROWS), 1)
    eye[...] = (rows_iota == cols_iota).astype(F32)
    row_m[...] = jnp.full((IMG, 128), -jnp.inf, F32)
    row_s[...] = jnp.zeros((IMG, 128), F32)

    def split_rows(src, n, high, low, at):
        def body(b, carry):
            r = pl.ds(pl.multiple_of(b * 32, 32), 32)
            o = pl.ds(pl.multiple_of(at + b * 32, 32), 32)
            v = src[n, r, :]
            h = v.astype(BF16)
            high[o, :] = h
            low[o, :] = (v - h.astype(F32)).astype(BF16)
            return carry

        lax.fori_loop(0, ROWS // 32, body, 0)

    w.wait(("S", 0))
    w.wait(("S", 1))
    w.wait(("S", 2))
    w.wait(("I", 3, 0))
    w.wait(("I", 3, 1))
    w.send(Ib.at[6], ("S", 3), sib)
    w.wait(("S", 3))

    def split_img(n, carry):
        split_rows(Ib, n, Ih, Il, n * ROWS)
        return carry

    lax.fori_loop(0, 8, split_img, 0)

    s2 = scale_ref[0] * LOG2E

    def block_of(qz, qy):
        return ((z + step_of(qz)) % 4) * 4 + (y + step_of(qy)) % 4

    def tile(n, carry):
        for m in range(8):

            @pl.when(n == m)
            def _():
                if m in (2, 3, 4):
                    second_ring((0, 0, 1, 2, 3)[m])
                qz, e = m // 2, m % 2
                for qy in (2 * e, 2 * e + 1):
                    for key in list(w.arrivals):
                        if key[0] in "AB" and key[1:3] == (qz, qy):
                            w.wait(key)

        cols = pl.ds(pl.multiple_of(n * 256, 256), 256)
        split_rows(Tb, 2 * n, Th, Tl, n * 256)
        split_rows(Tb, 2 * n + 1, Th, Tl, n * 256 + ROWS)
        L[:, cols] = s2 * dot3(Ih[...], Il[...], Th[cols, :], Tl[cols, :], 1, 1)

        def peak(b, top):
            r = pl.ds(pl.multiple_of(b * ROWS, ROWS), ROWS)
            v = L[r, cols]
            v0, v1 = v[:, :128], v[:, 128:]
            old = row_m[r, :]
            new = jnp.maximum(old, jnp.maximum(v0, v1))
            row_s[r, :] = row_s[r, :] * jnp.exp2(old - new) + (jnp.exp2(v0 - new) + jnp.exp2(v1 - new))
            row_m[r, :] = new
            return jnp.maximum(top, jnp.max(v.reshape(ROWS // 8, 8, 256), axis=0))

        top = lax.fori_loop(0, 8, peak, jnp.full((8, 256), -jnp.inf, F32))

        def total(b, s):
            r = pl.ds(pl.multiple_of(b * ROWS, ROWS), ROWS)
            v = L[r, cols].reshape(ROWS // 8, 8, 256)
            return s + jnp.sum(jnp.exp2(v - top[None]), axis=0)

        s8 = lax.fori_loop(0, 8, total, jnp.zeros((8, 256), F32))
        m1 = jnp.max(top, axis=0, keepdims=True)
        s1 = jnp.sum(s8 * jnp.exp2(top - m1), axis=0, keepdims=True)
        qz, e = n // 2, n % 2
        for j in range(2):
            at = pl.ds(block_of(qz, 2 * e + j), 1)
            cst[0, 0, at, :] = m1[:, 128 * j : 128 * j + 128]
            cst[0, 1, at, :] = s1[:, 128 * j : 128 * j + 128]
        return carry

    lax.fori_loop(0, 8, tile, 0)

    def img_block(s):
        return ((x + step_of(s // 2)) % 4) * 2 + (k + s % 2) % 2

    def fold_rows(s, carry):
        r = pl.ds(pl.multiple_of(s * ROWS, ROWS), ROWS)
        mt, st = row_m[r, :].T, row_s[r, :].T
        m1 = jnp.max(mt, axis=0, keepdims=True)
        s1 = jnp.sum(st * jnp.exp2(mt - m1), axis=0, keepdims=True)
        at = pl.ds(img_block(s), 1)
        rst[0, 0, at, :] = m1
        rst[0, 1, at, :] = s1
        return carry

    lax.fori_loop(0, 8, fold_rows, 0)
    w.flush(like)
    assert not w.arrivals

    w.open("r1", rst, 1)
    for n, d in enumerate((1, -1, 2)):
        w.open(("c1", d), cst, 1 + n)
        w.open(("r2", d), rst, 3 + n)
        w.open(("c2", d), cst, 5 + n)
    w.send(rst.at[0], "r1", sib)
    for d in (1, -1, 2):
        w.send(cst.at[0], ("c1", d), ys[d])
    w.wait("r1")
    m, s = merge([(rst[n, 0], rst[n, 1]) for n in (0, 1)])
    rst[2, 0], rst[2, 1] = m, s
    for d in (1, -1, 2):
        w.send(rst.at[2], ("r2", d), xs[d])
    for d in (1, -1, 2):
        w.wait(("c1", d))
    m, s = merge([(cst[n, 0], cst[n, 1]) for n in range(4)])
    cst[4, 0], cst[4, 1] = m, s
    for d in (1, -1, 2):
        w.send(cst.at[4], ("c2", d), zs[d])
    for d in (1, -1, 2):
        w.wait(("r2", d))
    m, s = merge([(rst[n, 0], rst[n, 1]) for n in range(2, 6)])
    row_lse = m + jnp.log2(s)
    for d in (1, -1, 2):
        w.wait(("c2", d))
    m, s = merge([(cst[n, 0], cst[n, 1]) for n in range(4, 8)])
    col_lse = m + jnp.log2(s)
    w.flush(like)
    rst[6, 0] = row_lse + 1.0
    cst[8, 0] = col_lse + 1.0
    acc[...] = jnp.full((8, 128), LN2 * (jnp.sum(row_lse) / 8 + jnp.sum(col_lse) / 16), F32)

    def spread(s, carry):
        r = pl.ds(pl.multiple_of(s * ROWS, ROWS), ROWS)
        v = rst[6, 0, pl.ds(img_block(s), 1), :]
        row_m[r, :] = jnp.broadcast_to(v, (ROWS, 128)).T
        return carry

    lax.fori_loop(0, 8, spread, 0)

    for q in range(4):
        w.open(("AP", q), tland, q)
        w.open(("BP", q), tland, 4 + q)
        for n, d in enumerate((1, -1)):
            w.open(("AD", q, d), Ib, q, pl.ds(HALF * n, HALF))
            w.open(("BD", q, d), Ib, 4 + q, pl.ds(HALF * n, HALF))
    for n, d in enumerate((1, -1)):
        w.open(("A2", d), tland, 8 + n)
        w.open(("B2", d), tland, 10 + n)
        w.open(("A2P", d), tland, 12, pl.ds(32 * n, 32))
        w.open(("B2P", d), tland, 13, pl.ds(32 * n, 32))
        w.open(("ID", d), iland, 4 + n)
        w.open(("IP", d), iland, 6, pl.ds(HALF * n, HALF))
    for q in range(4):
        w.open(("IS", q), iland, q)
    w.open("ls", lbuf, 1)
    for n, d in enumerate((1, -1, 2)):
        w.open(("lx", d), lbuf, 3 + n)
        w.open(("ly", d), lbuf, 7 + n)
        w.open(("lz", d), lbuf, 11 + n)

    def add(dst, srcs, rows, out=None, mul=None):
        step = 16

        def body(b, carry):
            r = pl.ds(pl.multiple_of(b * step, step), step)
            v = dst[r, :]
            for src in srcs:
                v = v + src[r, :]
            if out is None:
                dst[r, :] = v
            else:
                out[r, :] = mul * v
            return carry

        lax.fori_loop(0, rows // step, body, 0)

    def TA(qz, qy):
        return Tb.at[qz * 4 + qy, lo]

    def TB(qz, qy):
        return Tb.at[qz * 4 + qy, hi]

    def first_ring(name, q1, q2):
        nbr = zs if name == "A" else ys
        ref = TA(q1, q2) if name == "A" else TB(q2, q1)
        plus = q2 in (0, 3)
        if q1 == 3:
            if plus:
                w.send(ref, (name + "P", q2), nbr[-1])
            else:
                w.send(ref, (name + "P", q2), nbr[1])
        elif q1 == 2:
            if plus:
                add(ref, [w.wait((name + "P", q2))], HALF)
            w.send(ref, (name + "D", q2, 1), nbr[-1])
        elif q1 == 1:
            if not plus:
                add(ref, [w.wait((name + "P", q2))], HALF)
            w.send(ref, (name + "D", q2, -1), nbr[1])

    def second(name, q2):
        nbr = ys if name == "A" else zs
        ref = TA(0, q2) if name == "A" else TB(q2, 0)
        add(ref, [w.wait((name + "D", q2, 1)), w.wait((name + "D", q2, -1))], HALF)
        if q2 == 3:
            w.send(ref.at[pl.ds(0, 32)], (name + "2P", 1), nbr[-1])
            w.send(ref.at[pl.ds(32, 32)], (name + "2P", -1), nbr[1])
        elif q2 == 2:
            add(ref.at[pl.ds(0, 32)], [w.wait((name + "2P", 1))], 32)
            w.send(ref, (name + "2", 1), nbr[-1])
        elif q2 == 1:
            add(ref.at[pl.ds(32, 32)], [w.wait((name + "2P", -1))], 32)
            w.send(ref, (name + "2", -1), nbr[1])
        else:
            at = lo if name == "A" else hi
            srcs = [w.wait((name + "2", 1)), w.wait((name + "2", -1))]
            add(ref, srcs, HALF, txt_out.at[at], scale_ref[0])

    def text_events(n):
        if n == 1:
            for q in (3, 0, 1, 2):
                first_ring("A", 3, q)
            first_ring("B", 3, 3)
            first_ring("B", 1, 3)
        if n == 3:
            for q in (1, 2):
                first_ring("A", 2, q)
            first_ring("B", 3, 2)
            first_ring("B", 2, 2)
            first_ring("B", 2, 3)
        if n == 5:
            for q in (3, 0):
                first_ring("A", 1, q)
            first_ring("B", 3, 1)
            first_ring("B", 2, 1)
            first_ring("A", 2, 3)
            first_ring("A", 2, 0)
            first_ring("A", 1, 1)
            first_ring("A", 1, 2)
            first_ring("B", 1, 2)
        if n == 7:
            first_ring("B", 3, 0)
            first_ring("B", 1, 0)
            first_ring("B", 1, 1)
            second("B", 3)

    dsum = jnp.zeros((8, 128), F32)
    lbuf[0] = dsum

    def text_step(n, carry):
        p = 7 - n
        qz, e = p // 2, p % 2
        cols = pl.ds(pl.multiple_of(p * 256, 256), 256)
        blocks = [block_of(qz, 2 * e + j) for j in range(2)]
        cl = jnp.concatenate([cst[8, 0, pl.ds(b, 1), :] for b in blocks], axis=1)

        def soft(b, inner):
            r = pl.ds(pl.multiple_of(b * 64, 64), 64)
            v = L[r, cols]
            rl = row_m[r, :]
            g = jnp.exp2(v - jnp.concatenate([rl, rl], axis=1)) + jnp.exp2(v - cl)
            h = g.astype(BF16)
            Ph[r, cols] = h
            Pl[r, cols] = (g - h.astype(F32)).astype(BF16)
            return inner

        lax.fori_loop(0, IMG // 64, soft, 0)
        for j in range(2):
            there = t * 16 + blocks[j] - i * 8

            @pl.when((there >= 0) & (there < 8))
            def _():
                d = (there // 2 + 4 - x) % 4
                s = step_of(d) * 2 + (there % 2 + k) % 2
                r = pl.ds(pl.multiple_of(s * ROWS, ROWS), ROWS)
                c = pl.ds(pl.multiple_of(p * 256 + j * 128, 128), 128)
                v = L[r, c]
                g = jnp.exp2(v - row_m[r, :]) + jnp.exp2(v - cl[:, 128 * j : 128 * j + 128]) - eye[...]
                h = g.astype(BF16)
                Ph[r, c] = h
                Pl[r, c] = (g - h.astype(F32)).astype(BF16)
                lbuf[0] += jnp.sum((v * eye[...]).reshape(ROWS // 8, 8, 128), axis=0)

        res = dot3(Ph[:, cols], Pl[:, cols], Ih[...], Il[...], 0, 0)
        Tb[2 * p] = res[:ROWS]
        Tb[2 * p + 1] = res[ROWS:]
        for m in range(8):

            @pl.when(n == m)
            def _():
                text_events(m)

        return carry

    lax.fori_loop(0, 8, text_step, 0)
    total = jnp.sum(acc[...]) / 1024 - 2.0 * LN2 * jnp.sum(lbuf[0])
    lbuf[0] = jnp.full((8, 128), total, F32)
    w.send(lbuf.at[0], "ls", sib)

    def iref(s):
        return L.at[pl.ds(s * ROWS, ROWS), pl.ds(0, E)]

    def image_events(m):
        q = 3 - m
        w.send(iref(2 * q + 1), ("IS", q), sib)
        if m == 0:
            first_ring("B", 2, 0)
            second("B", 2)
            second("A", 3)
        if m == 1:
            second("B", 1)
            second("A", 2)
            second("A", 1)
        mine = iref(2 * q)
        add(mine, [w.wait(("IS", q))], ROWS)
        if m == 0:
            w.send(mine.at[lo], ("IP", 1), xs[-1])
            w.send(mine.at[hi], ("IP", -1), xs[1])
        elif m == 1:
            add(mine.at[lo], [w.wait(("IP", 1))], HALF)
            w.send(mine, ("ID", 1), xs[-1])
        elif m == 2:
            add(mine.at[hi], [w.wait(("IP", -1))], HALF)
            w.send(mine, ("ID", -1), xs[1])
        if m == 0:
            w.wait("ls")
            lbuf[2] = lbuf[0] + lbuf[1]
            for d in (1, -1, 2):
                w.send(lbuf.at[2], ("lx", d), xs[d])
        elif m < 3:
            a, b, nbr, base = (("lx", "ly", ys, 2), ("ly", "lz", zs, 6))[m - 1]
            for d in (1, -1, 2):
                w.wait((a, d))
            lbuf[base + 4] = (lbuf[base] + lbuf[base + 1]) + (lbuf[base + 2] + lbuf[base + 3])
            for d in (1, -1, 2):
                w.send(lbuf.at[base + 4], (b, d), nbr[d])

    def image_step(m, carry):
        r = pl.ds(pl.multiple_of((3 - m) * 256, 256), 256)
        L[r, 0:E] = dot3(Ph[r, :], Pl[r, :], Th[...], Tl[...], 1, 0)
        for n in range(4):

            @pl.when(m == n)
            def _():
                image_events(n)

        return carry

    lax.fori_loop(0, 4, image_step, 0)
    second("A", 0)
    second("B", 0)
    add(iref(0), [w.wait(("ID", 1)), w.wait(("ID", -1))], ROWS, img_out, scale_ref[0])
    for d in (1, -1, 2):
        w.wait(("lz", d))
    loss_ref[...] = ((lbuf[10] + lbuf[11]) + (lbuf[12] + lbuf[13])) / (2.0 * 16384)
    w.flush(like)
    assert not w.arrivals


def on_device(image_emb, text_emb, logit_scale):
    vm = pltpu.VMEM
    loss, image_grad, text_grad = pl.pallas_call(
        kernel,
        out_shape=(
            jax.ShapeDtypeStruct((8, 128), F32),
            jax.ShapeDtypeStruct((ROWS, E), F32),
            jax.ShapeDtypeStruct((ROWS, E), F32),
        ),
        in_specs=[
            pl.BlockSpec(memory_space=pltpu.SMEM),
            pl.BlockSpec(memory_space=pl.ANY),
            pl.BlockSpec(memory_space=pl.ANY),
        ],
        out_specs=[pl.BlockSpec(memory_space=vm)] * 3,
        scratch_shapes=[
            vm((8, ROWS, E), F32),
            vm((16, ROWS, E), F32),
            vm((IMG, E), BF16),
            vm((IMG, E), BF16),
            vm((TXT, E), BF16),
            vm((TXT, E), BF16),
            vm((IMG, TXT), F32),
            vm((IMG, TXT), BF16),
            vm((IMG, TXT), BF16),
            vm((IMG, 128), F32),
            vm((IMG, 128), F32),
            vm((7, 2, 8, 128), F32),
            vm((9, 2, 16, 128), F32),
            vm((8, 128), F32),
            vm((14, 8, 128), F32),
            vm((14, HALF, E), F32),
            vm((7, ROWS, E), F32),
            vm((ROWS, ROWS), F32),
            pltpu.SemaphoreType.DMA((56,)),
            pltpu.SemaphoreType.DMA((112,)),
            pltpu.SemaphoreType.DMA((2,)),
        ],
        compiler_params=pltpu.CompilerParams(
            collective_id=0, has_side_effects=True, vmem_limit_bytes=63 * 2**20
        ),
        name="contrastive",
    )(logit_scale.reshape(1), image_emb, text_emb)
    return loss[0, 0], image_grad, text_grad


def solution(mesh):
    in_specs = (P(("img", "txt"), None), P(("txt", "img"), None), P())
    out_specs = (P(), P(("img", "txt"), None), P(("txt", "img"), None))
    return jax.shard_map(
        on_device, mesh=mesh, in_specs=in_specs, out_specs=out_specs, check_vma=False
    )
```

time: 581 us -> 184 us (0.32)
  waiting for transfers between devices: 251 us -> 0 us
  Pallas kernels: 0 us -> 178 us
  blocking collectives: 166 us -> 0 us
  matrix products: 129 us -> 0 us
  between operations: 18.2 us -> 1.29 us
  other arithmetic: 13 us -> 0 us
    pallas_call x0 -> x1, Pallas kernels: none -> 178 us  [on_device(): pl.pallas_call(kernel, out_shape=(jax.ShapeDtypeStruct((8, 128), F32), ja...]
    dot_general x3 -> x0, matrix products: 129 us -> none  [the longest x1 45.1 us: on_device(): lax.dot_general(img_rows, txt_cols, (((1,), (1,)), ((), ())), precision=l...]
    psum x2 -> x0, waiting for transfers between devices: 126 us -> none  [the longest x1 126 us: on_device(): text_whole = lax.psum(text_part, 'img')]
    all_gather x2 -> x0, waiting for transfers between devices: 123 us -> none  [the longest x1 82.3 us: on_device(): txt_cols = lax.all_gather(text_emb, 'img', axis=0, tiled=True)]
    psum x3 -> x0, blocking collectives: 122 us -> none  [the longest x1 77.9 us: on_device(): summed_loss = lax.psum(local_part, ('img', 'txt'))]
    pmax x2 -> x0, blocking collectives: 44.4 us -> none  [the longest x1 32 us: on_device(): col_peak = lax.pmax(jnp.max(logits, axis=0), 'img')]
    reduce_sum x4 -> x0, other arithmetic: 13 us -> none  [the longest x1 6.99 us: on_device(): diagonal_sum = jnp.sum(logits * diagonal_mask)]
  transfers between devices with their start and end apart: 4 -> 0, of which waited for: 3 -> 0; matrix products, arithmetic and copies ran while one was open for 7% -> 0% of each run, Pallas kernels for 0% -> 0%
where the time goes in v1:
time: 184 us; the launch traced here: 183 us
  Pallas kernels  178 us (97%)
  local copies, waits for them, and re-layouts  4.06 us (2%)
    pallas_call x1, Pallas kernels, on_device(): pl.pallas_call(kernel, out_shape=(jax.ShapeDtypeStruct((8, 128), F32), ja...  178 us

profile of v1, /device:TPU:1, one launch (start us, length us, event | category | flops | bytes accessed | tf_op | source)
XLA Modules:
  0.0 183.4 jit_solution(646340835001699877)
XLA Ops:
  1.3 178.0 %contrastive.1 = (f32[8,128]{1,0:T(8,128)}, f32[128,1280]{1,0:T(8,128)}, f32[128,1280]{1,0:T(8,128)}) custom-call(f32[1]{0:T(128)} %bitcast.2.scale_ref, f32[128,1280]{1,0:T(8,128)} %img_ref.1, f32[128,1280]{1,0:T(8,128)} %txt_ref.1), custom_call_target="tpu_custom_call" | custom-call | tf_op jit(solution)/shard_map/contrastive/pallas_call | solution.py:546
  179.3 1.2 slice.3
  180.5 0.0 copy-start
  180.5 2.0 %copy.9 = f32[128,1280]{1,0:T(8,128)} copy(f32[128,1280]{1,0:T(8,128)} %get-tuple-element.13) | data formatting | bytes 1310720
  182.5 0.0 copy-done
  182.5 0.8 copy.10
Async XLA Ops:
  180.5 2.0 %copy-start = (f32[128,1280]{1,0:T(8,128)S(1)}, f32[128,1280]{1,0:T(8,128)}, u32[]{:S(2)}) copy-start(f32[128,1280]{1,0:T(8,128)} %get-tuple-element.14) | copy-start | bytes 1966084

commit v2 on v1

--- a/solution.py
+++ b/solution.py
@@ -19,8 +19,47 @@
 IMG, TXT = 1024, 2048
 
 
-def step_of(q):
-    return q + q // 2 - 2 * (q // 3)
+PAIRS = (
+    ((0, 1), (0, 2)), ((1, 0), (2, 0)), ((1, 2), (0, 0)), ((0, 3), (1, 1)),
+    ((3, 0), (2, 3)), ((1, 3), (2, 1)), ((3, 2), (2, 2)), ((3, 3), (3, 1)),
+)
+SLOT = {where: 2 * n + j for n, pair in enumerate(PAIRS) for j, where in enumerate(pair)}
+
+GATHER = (
+    (("B", 1, 0), ("B", 2, 0), ("A", 0, 2), ("A", 0, 1), ("I", 1), ("I", 2), ("S", 0),
+     ("A", 2, 0), ("B", 0, 2), ("B", 0, 1), ("A", 1, 0)),
+    (("A", 1, 1), ("A", 0, 3, 1), ("B", 3, 0, 0), ("B", 1, 2), ("B", 2, 1), ("A", 2, 1), ("B", 3, 0, 1),
+     ("A", 0, 3, 0), ("I", 3, 0), ("S", 1), ("S", 2), ("I", 3, 1), ("A", 3, 0), ("B", 0, 3), ("B", 1, 1), ("A", 1, 2)),
+    (),
+    (("S", 3), ("A", 1, 3), ("A", 2, 3), ("B", 3, 2), ("B", 2, 3)),
+    (), (),
+    (("B", 1, 3), ("A", 3, 2), ("B", 2, 2), ("A", 2, 2)),
+    (),
+    (("A", 3, 3), ("B", 3, 1), ("B", 3, 3), ("A", 3, 1)),
+    (), (), (), (),
+)
+
+STEPS = (("t", 0), ("t", 1), ("t", 2), ("t", 3), ("t", 4), ("t", 5),
+         ("i", 3), ("i", 2), ("i", 1), ("t", 6), ("t", 7), ("i", 0))
+RETURN = (
+    (("B", "P", 3), ("A", "P", 3), ("A", "P", 1), ("B", "D", 3, -1)),
+    (("A", "P", 2), ("B", "D", 2, 1), ("A", "D", 2, 1)),
+    (("B", "P", 1), ("B", "D", 3, 1), ("A", "D", 3, -1), ("A", "D", 1, 1)),
+    (("B", "P", 2),),
+    (),
+    (("A", "D", 3, 1), ("B", "P", 0), ("A", "D", 2, -1)),
+    (("IS", 3), ("B", "D", 1, 1), ("B", "D", 1, -1), ("A", "P", 0), ("A", "D", 1, -1)),
+    (("IP", 1), ("IP", -1), ("IS", 2), ("B", "D", 2, -1)),
+    (("IS", 1), ("B", "2P", 1), ("B", "2P", -1), ("A", "2P", 1), ("A", "2P", -1)),
+    (("A", "D", 0, -1),),
+    (("ID", 1), ("ID", -1), ("B", "D", 0, 1), ("B", "D", 0, -1), ("B", "2", 1), ("B", "2", -1),
+     ("A", "2", 1), ("A", "D", 0, 1)),
+    (("A", "2", -1), ("IS", 0), ("B", "F"), ("IF",), ("A", "F")),
+)
+
+
+def pick(n, values):
+    return sum(jnp.where(n == j, v, 0) for j, v in enumerate(values))
 
 
 def dot(a, b, ca, cb):
@@ -61,6 +100,11 @@
         pltpu.make_async_copy(dst, dst, self.recv_sem.at[n]).wait()
         return dst
 
+    def need(self, *keys):
+        for key in keys:
+            if key in self.arrivals:
+                self.wait(key)
+
     def flush(self, like):
         for s, shape in enumerate(self.sent):
             ref = like(shape)
@@ -108,7 +152,7 @@
     lo, hi = pl.ds(0, HALF), pl.ds(HALF, HALF)
 
     def T(qz, qy, part):
-        return Tb.at[qz * 4 + qy, part]
+        return Tb.at[SLOT[qz, qy], part]
 
     for qz in range(4):
         for qy in range(4):
@@ -117,10 +161,10 @@
                     continue
                 if split:
                     at = 0 if name == "A" else HALF
-                    w.open((name, qz, qy, 0), Tb, qz * 4 + qy, pl.ds(at, 32))
-                    w.open((name, qz, qy, 1), Tb, qz * 4 + qy, pl.ds(at + 32, 32))
+                    w.open((name, qz, qy, 0), Tb, SLOT[qz, qy], pl.ds(at, 32))
+                    w.open((name, qz, qy, 1), Tb, SLOT[qz, qy], pl.ds(at + 32, 32))
                 else:
-                    w.open((name, qz, qy), Tb, qz * 4 + qy, part)
+                    w.open((name, qz, qy), Tb, SLOT[qz, qy], part)
     for q in (1, 2):
         w.open(("I", q), Ib, 2 * q)
     w.open(("I", 3, 0), Ib, 6, lo)
@@ -128,58 +172,55 @@
     for q in range(4):
         w.open(("S", q), Ib, 2 * q + 1)
 
-    own_t = pltpu.make_async_copy(txt_ref, Tb.at[0], local_sem.at[0])
+    def text_keys(qz, qy):
+        return [(n, qz, qy, *h) for n in "AB" for h in ((), (0,), (1,))]
+
+    def gather_send(key):
+        name, first = key[0], key[1]
+        if name == "S":
+            q = first
+            w.need(("I", q), ("I", 3, 0), ("I", 3, 1)) if q == 3 else w.need(("I", q))
+            w.send(img_ref if q == 0 else Ib.at[2 * q], key, sib)
+        elif name == "I":
+            if len(key) == 2:
+                w.send(img_ref, key, xs[1 if first == 2 else -1])
+            else:
+                q = 2 - key[2]
+                w.need(("I", q))
+                w.send(Ib.at[2 * q, (lo, hi)[key[2]]], key, xs[1 - 2 * key[2]])
+        else:
+            q1, q2 = (key[2], key[1]) if name == "A" else (key[1], key[2])
+            ring1, ring2 = (ys, zs) if name == "A" else (zs, ys)
+            at = 0 if name == "A" else HALF
+
+            def where(a, b):
+                return (b, a) if name == "A" else (a, b)
+
+            if len(key) == 4:
+                q = 2 - key[3]
+                w.need((name, *where(q, 0)))
+                w.send(T(*where(q, 0), pl.ds(at + 32 * key[3], 32)), key, ring1[1 - 2 * key[3]])
+            elif q2 == 0:
+                w.send(txt_ref.at[pl.ds(at, HALF)], key, ring1[1 if q1 == 2 else -1])
+            else:
+                if q2 == 3:
+                    q, d = (2, 1) if q1 in (0, 3) else (1, -1)
+                else:
+                    q, d = 0, (1 if q2 == 2 else -1)
+                source = where(q1, q)
+                if source == (0, 0):
+                    w.send(txt_ref.at[pl.ds(at, HALF)], key, ring2[d])
+                else:
+                    w.need(*[k for k in text_keys(*source) if k[0] == name])
+                    w.send(T(*source, pl.ds(at, HALF)), key, ring2[d])
+
+    own_t = pltpu.make_async_copy(txt_ref, Tb.at[SLOT[0, 0]], local_sem.at[0])
     own_i = pltpu.make_async_copy(img_ref, Ib.at[0], local_sem.at[1])
-    w.send(txt_ref.at[lo], ("A", 0, 2), ys[1])
-    w.send(txt_ref.at[lo], ("A", 0, 1), ys[-1])
-    w.send(txt_ref.at[hi], ("B", 2, 0), zs[1])
-    w.send(txt_ref.at[hi], ("B", 1, 0), zs[-1])
-    w.send(img_ref, ("I", 2), xs[1])
-    w.send(img_ref, ("I", 1), xs[-1])
-    w.send(txt_ref.at[lo], ("A", 2, 0), zs[1])
-    w.send(txt_ref.at[lo], ("A", 1, 0), zs[-1])
-    w.send(txt_ref.at[hi], ("B", 0, 2), ys[1])
-    w.send(txt_ref.at[hi], ("B", 0, 1), ys[-1])
-    w.send(img_ref, ("S", 0), sib)
+    for key in GATHER[0]:
+        gather_send(key)
     own_t.start()
     own_i.start()
 
-    for q, back in ((2, 1), (1, -1)):
-        part = 0 if q == 2 else 1
-        src = w.wait(("A", 0, q))
-        w.send(T(0, q, pl.ds(32 * part, 32)), ("A", 0, 3, part), ys[back])
-        w.send(src, ("A", 2, q), zs[1])
-        w.send(src, ("A", 1, q), zs[-1])
-        src = w.wait(("B", q, 0))
-        w.send(T(q, 0, pl.ds(HALF + 32 * part, 32)), ("B", 3, 0, part), zs[back])
-        w.send(src, ("B", q, 2), ys[1])
-        w.send(src, ("B", q, 1), ys[-1])
-    for q, back in ((2, 1), (1, -1)):
-        src = w.wait(("I", q))
-        part = 0 if q == 2 else 1
-        w.send(Ib.at[2 * q, pl.ds(HALF * part, HALF)], ("I", 3, part), xs[back])
-        w.send(src, ("S", q), sib)
-    for name, where, a, b in (("A", (0, 3), 2, 1), ("B", (3, 0), 2, 1)):
-        w.wait((name, *where, 0))
-        w.wait((name, *where, 1))
-        if name == "A":
-            w.send(T(0, 3, lo), ("A", 2, 3), zs[1])
-            w.send(T(0, 3, lo), ("A", 1, 3), zs[-1])
-        else:
-            w.send(T(3, 0, hi), ("B", 3, 2), ys[1])
-            w.send(T(3, 0, hi), ("B", 3, 1), ys[-1])
-
-    def second_ring(q):
-        if q in (0, 3):
-            w.send(w.wait(("A", 2, q)), ("A", 3, q), zs[1])
-            w.send(w.wait(("B", q, 2)), ("B", q, 3), ys[1])
-        else:
-            w.send(w.wait(("A", 1, q)), ("A", 3, q), zs[-1])
-            w.send(w.wait(("B", q, 1)), ("B", q, 3), ys[-1])
-
-    second_ring(0)
-    own_i.wait()
-    own_t.wait()
     rows_iota = lax.broadcasted_iota(jnp.int32, (ROWS, ROWS), 0)
     cols_iota = lax.broadcasted_iota(jnp.int32, (ROWS, ROWS), 1)
     eye[...] = (rows_iota == cols_iota).astype(F32)
@@ -198,37 +239,31 @@
 
         lax.fori_loop(0, ROWS // 32, body, 0)
 
-    w.wait(("S", 0))
-    w.wait(("S", 1))
-    w.wait(("S", 2))
-    w.wait(("I", 3, 0))
-    w.wait(("I", 3, 1))
-    w.send(Ib.at[6], ("S", 3), sib)
-    w.wait(("S", 3))
-
-    def split_img(n, carry):
-        split_rows(Ib, n, Ih, Il, n * ROWS)
-        return carry
-
-    lax.fori_loop(0, 8, split_img, 0)
+    own_i.wait()
+    for q in range(4):
+        if q > 0:
+            for key in GATHER[q]:
+                gather_send(key)
+        w.need(("I", q), ("S", q), *([("I", 3, 0), ("I", 3, 1)] if q == 3 else []))
+        split_rows(Ib, 2 * q, Ih, Il, 2 * q * ROWS)
+        split_rows(Ib, 2 * q + 1, Ih, Il, (2 * q + 1) * ROWS)
+    own_t.wait()
 
     s2 = scale_ref[0] * LOG2E
-
-    def block_of(qz, qy):
-        return ((z + step_of(qz)) % 4) * 4 + (y + step_of(qy)) % 4
+    held = [((z + STEP[qz]) % 4) * 4 + (y + STEP[qy]) % 4 for pair in PAIRS for qz, qy in pair]
+
+    def blocks_of(n):
+        return [pick(n, held[j::2]) for j in range(2)]
 
     def tile(n, carry):
         for m in range(8):
 
             @pl.when(n == m)
             def _():
-                if m in (2, 3, 4):
-                    second_ring((0, 0, 1, 2, 3)[m])
-                qz, e = m // 2, m % 2
-                for qy in (2 * e, 2 * e + 1):
-                    for key in list(w.arrivals):
-                        if key[0] in "AB" and key[1:3] == (qz, qy):
-                            w.wait(key)
+                for key in GATHER[4 + m]:
+                    gather_send(key)
+                for where in PAIRS[m]:
+                    w.need(*text_keys(*where))
 
         cols = pl.ds(pl.multiple_of(n * 256, 256), 256)
         split_rows(Tb, 2 * n, Th, Tl, n * 256)
@@ -255,14 +290,16 @@
         s8 = lax.fori_loop(0, 8, total, jnp.zeros((8, 256), F32))
         m1 = jnp.max(top, axis=0, keepdims=True)
         s1 = jnp.sum(s8 * jnp.exp2(top - m1), axis=0, keepdims=True)
-        qz, e = n // 2, n % 2
-        for j in range(2):
-            at = pl.ds(block_of(qz, 2 * e + j), 1)
+        for j, block in enumerate(blocks_of(n)):
+            at = pl.ds(block, 1)
             cst[0, 0, at, :] = m1[:, 128 * j : 128 * j + 128]
             cst[0, 1, at, :] = s1[:, 128 * j : 128 * j + 128]
         return carry
 
     lax.fori_loop(0, 8, tile, 0)
+
+    def step_of(q):
+        return q + q // 2 - 2 * (q // 3)
 
     def img_block(s):
         return ((x + step_of(s // 2)) % 4) * 2 + (k + s % 2) % 2
@@ -321,17 +358,15 @@
 
     lax.fori_loop(0, 8, spread, 0)
 
-    for q in range(4):
-        w.open(("AP", q), tland, q)
-        w.open(("BP", q), tland, 4 + q)
+    for base, name in enumerate("AB"):
+        for q in range(4):
+            w.open((name, "P", q), tland, 4 * base + q)
+            for n, d in enumerate((1, -1)):
+                w.open((name, "D", q, d), Ib, 4 * base + q, pl.ds(HALF * n, HALF))
         for n, d in enumerate((1, -1)):
-            w.open(("AD", q, d), Ib, q, pl.ds(HALF * n, HALF))
-            w.open(("BD", q, d), Ib, 4 + q, pl.ds(HALF * n, HALF))
+            w.open((name, "2", d), tland, 8 + 2 * base + n)
+            w.open((name, "2P", d), tland, 12 + base, pl.ds(32 * n, 32))
     for n, d in enumerate((1, -1)):
-        w.open(("A2", d), tland, 8 + n)
-        w.open(("B2", d), tland, 10 + n)
-        w.open(("A2P", d), tland, 12, pl.ds(32 * n, 32))
-        w.open(("B2P", d), tland, 13, pl.ds(32 * n, 32))
         w.open(("ID", d), iland, 4 + n)
         w.open(("IP", d), iland, 6, pl.ds(HALF * n, HALF))
     for q in range(4):
@@ -358,88 +393,77 @@
 
         lax.fori_loop(0, rows // step, body, 0)
 
-    def TA(qz, qy):
-        return Tb.at[qz * 4 + qy, lo]
-
-    def TB(qz, qy):
-        return Tb.at[qz * 4 + qy, hi]
-
-    def first_ring(name, q1, q2):
-        nbr = zs if name == "A" else ys
-        ref = TA(q1, q2) if name == "A" else TB(q2, q1)
-        plus = q2 in (0, 3)
-        if q1 == 3:
-            if plus:
-                w.send(ref, (name + "P", q2), nbr[-1])
-            else:
-                w.send(ref, (name + "P", q2), nbr[1])
-        elif q1 == 2:
-            if plus:
-                add(ref, [w.wait((name + "P", q2))], HALF)
-            w.send(ref, (name + "D", q2, 1), nbr[-1])
-        elif q1 == 1:
-            if not plus:
-                add(ref, [w.wait((name + "P", q2))], HALF)
-            w.send(ref, (name + "D", q2, -1), nbr[1])
-
-    def second(name, q2):
-        nbr = ys if name == "A" else zs
-        ref = TA(0, q2) if name == "A" else TB(q2, 0)
-        add(ref, [w.wait((name + "D", q2, 1)), w.wait((name + "D", q2, -1))], HALF)
-        if q2 == 3:
-            w.send(ref.at[pl.ds(0, 32)], (name + "2P", 1), nbr[-1])
-            w.send(ref.at[pl.ds(32, 32)], (name + "2P", -1), nbr[1])
-        elif q2 == 2:
-            add(ref.at[pl.ds(0, 32)], [w.wait((name + "2P", 1))], 32)
-            w.send(ref, (name + "2", 1), nbr[-1])
-        elif q2 == 1:
-            add(ref.at[pl.ds(32, 32)], [w.wait((name + "2P", -1))], 32)
-            w.send(ref, (name + "2", -1), nbr[1])
+    summed = set()
+
+    def text_send(key):
+        name, kind = key[0], key[1]
+        ring1, ring2 = (zs, ys) if name == "A" else (ys, zs)
+        part = lo if name == "A" else hi
+
+        def ref(q1, q2, rows=None):
+            qz, qy = (q1, q2) if name == "A" else (q2, q1)
+            at = (0 if name == "A" else HALF) + (rows or 0)
+            return Tb.at[SLOT[qz, qy], pl.ds(at, HALF if rows is None else 32)]
+
+        def first_sum(q2):
+            if (name, q2) not in summed:
+                summed.add((name, q2))
+                add(ref(0, q2), [w.wait((name, "D", q2, 1)), w.wait((name, "D", q2, -1))], HALF)
+
+        if kind == "P":
+            q2 = key[2]
+            w.send(ref(3, q2), key, ring1[-1 if q2 in (0, 3) else 1])
+        elif kind == "D":
+            q2, d = key[2], key[3]
+            mine = ref(2 if d == 1 else 1, q2)
+            if (d == 1) == (q2 in (0, 3)):
+                add(mine, [w.wait((name, "P", q2))], HALF)
+            w.send(mine, key, ring1[-d])
+        elif kind == "2P":
+            d = key[2]
+            first_sum(3)
+            w.send(ref(0, 3, 0 if d == 1 else 32), key, ring2[-d])
+        elif kind == "2":
+            d = key[2]
+            q2 = 2 if d == 1 else 1
+            first_sum(q2)
+            add(ref(0, q2, 0 if d == 1 else 32), [w.wait((name, "2P", d))], 32)
+            w.send(ref(0, q2), key, ring2[-d])
         else:
-            at = lo if name == "A" else hi
-            srcs = [w.wait((name + "2", 1)), w.wait((name + "2", -1))]
-            add(ref, srcs, HALF, txt_out.at[at], scale_ref[0])
-
-    def text_events(n):
-        if n == 1:
-            for q in (3, 0, 1, 2):
-                first_ring("A", 3, q)
-            first_ring("B", 3, 3)
-            first_ring("B", 1, 3)
-        if n == 3:
-            for q in (1, 2):
-                first_ring("A", 2, q)
-            first_ring("B", 3, 2)
-            first_ring("B", 2, 2)
-            first_ring("B", 2, 3)
-        if n == 5:
-            for q in (3, 0):
-                first_ring("A", 1, q)
-            first_ring("B", 3, 1)
-            first_ring("B", 2, 1)
-            first_ring("A", 2, 3)
-            first_ring("A", 2, 0)
-            first_ring("A", 1, 1)
-            first_ring("A", 1, 2)
-            first_ring("B", 1, 2)
-        if n == 7:
-            first_ring("B", 3, 0)
-            first_ring("B", 1, 0)
-            first_ring("B", 1, 1)
-            second("B", 3)
-
-    dsum = jnp.zeros((8, 128), F32)
-    lbuf[0] = dsum
-
-    def text_step(n, carry):
+            srcs = [w.wait((name, "D", 0, 1)), w.wait((name, "D", 0, -1)), w.wait((name, "2", 1)), w.wait((name, "2", -1))]
+            add(ref(0, 0), srcs, HALF, txt_out.at[part], scale_ref[0])
+
+    def iref(s):
+        return L.at[pl.ds(s * ROWS, ROWS), pl.ds(0, E)]
+
+    def image_send(key):
+        kind = key[0]
+        if kind == "IS":
+            w.send(iref(2 * key[1] + 1), key, sib)
+        elif kind == "IP":
+            if "i3" not in summed:
+                summed.add("i3")
+                add(iref(6), [w.wait(("IS", 3))], ROWS)
+            w.send(iref(6).at[lo if key[1] == 1 else hi], key, xs[-key[1]])
+        elif kind == "ID":
+            d = key[1]
+            q = 2 if d == 1 else 1
+            add(iref(2 * q), [w.wait(("IS", q))], ROWS)
+            add(iref(2 * q).at[lo if d == 1 else hi], [w.wait(("IP", d))], HALF)
+            w.send(iref(2 * q), key, xs[-d])
+        else:
+            add(iref(0), [w.wait(("IS", 0)), w.wait(("ID", 1)), w.wait(("ID", -1))], ROWS, img_out, scale_ref[0])
+
+    lbuf[0] = jnp.zeros((8, 128), F32)
+
+    def soften(n, carry):
         p = 7 - n
-        qz, e = p // 2, p % 2
         cols = pl.ds(pl.multiple_of(p * 256, 256), 256)
-        blocks = [block_of(qz, 2 * e + j) for j in range(2)]
+        blocks = blocks_of(p)
         cl = jnp.concatenate([cst[8, 0, pl.ds(b, 1), :] for b in blocks], axis=1)
 
         def soft(b, inner):
-            r = pl.ds(pl.multiple_of(b * 64, 64), 64)
+            r = pl.ds(pl.multiple_of(b * ROWS, ROWS), ROWS)
             v = L[r, cols]
             rl = row_m[r, :]
             g = jnp.exp2(v - jnp.concatenate([rl, rl], axis=1)) + jnp.exp2(v - cl)
@@ -448,7 +472,7 @@
             Pl[r, cols] = (g - h.astype(F32)).astype(BF16)
             return inner
 
-        lax.fori_loop(0, IMG // 64, soft, 0)
+        lax.fori_loop(0, IMG // ROWS, soft, 0)
         for j in range(2):
             there = t * 16 + blocks[j] - i * 8
 
@@ -465,75 +489,55 @@
                 Pl[r, c] = (g - h.astype(F32)).astype(BF16)
                 lbuf[0] += jnp.sum((v * eye[...]).reshape(ROWS // 8, 8, 128), axis=0)
 
-        res = dot3(Ph[:, cols], Pl[:, cols], Ih[...], Il[...], 0, 0)
-        Tb[2 * p] = res[:ROWS]
-        Tb[2 * p + 1] = res[ROWS:]
-        for m in range(8):
-
-            @pl.when(n == m)
-            def _():
-                text_events(m)
-
         return carry
 
-    lax.fori_loop(0, 8, text_step, 0)
-    total = jnp.sum(acc[...]) / 1024 - 2.0 * LN2 * jnp.sum(lbuf[0])
-    lbuf[0] = jnp.full((8, 128), total, F32)
-    w.send(lbuf.at[0], "ls", sib)
-
-    def iref(s):
-        return L.at[pl.ds(s * ROWS, ROWS), pl.ds(0, E)]
-
-    def image_events(m):
-        q = 3 - m
-        w.send(iref(2 * q + 1), ("IS", q), sib)
-        if m == 0:
-            first_ring("B", 2, 0)
-            second("B", 2)
-            second("A", 3)
+    def loss_send(m):
         if m == 1:
-            second("B", 1)
-            second("A", 2)
-            second("A", 1)
-        mine = iref(2 * q)
-        add(mine, [w.wait(("IS", q))], ROWS)
-        if m == 0:
-            w.send(mine.at[lo], ("IP", 1), xs[-1])
-            w.send(mine.at[hi], ("IP", -1), xs[1])
-        elif m == 1:
-            add(mine.at[lo], [w.wait(("IP", 1))], HALF)
-            w.send(mine, ("ID", 1), xs[-1])
-        elif m == 2:
-            add(mine.at[hi], [w.wait(("IP", -1))], HALF)
-            w.send(mine, ("ID", -1), xs[1])
-        if m == 0:
+            total = jnp.sum(acc[...]) / 1024 - 2.0 * LN2 * jnp.sum(lbuf[0])
+            lbuf[0] = jnp.full((8, 128), total, F32)
+            w.send(lbuf.at[0], "ls", sib)
+        if m == 3:
             w.wait("ls")
             lbuf[2] = lbuf[0] + lbuf[1]
             for d in (1, -1, 2):
                 w.send(lbuf.at[2], ("lx", d), xs[d])
-        elif m < 3:
-            a, b, nbr, base = (("lx", "ly", ys, 2), ("ly", "lz", zs, 6))[m - 1]
+        if m in (5, 7):
+            a, b, nbr, base = ("lx", "ly", ys, 2) if m == 5 else ("ly", "lz", zs, 6)
             for d in (1, -1, 2):
                 w.wait((a, d))
             lbuf[base + 4] = (lbuf[base] + lbuf[base + 1]) + (lbuf[base + 2] + lbuf[base + 3])
             for d in (1, -1, 2):
                 w.send(lbuf.at[base + 4], (b, d), nbr[d])
 
-    def image_step(m, carry):
-        r = pl.ds(pl.multiple_of((3 - m) * 256, 256), 256)
-        L[r, 0:E] = dot3(Ph[r, :], Pl[r, :], Th[...], Tl[...], 1, 0)
-        for n in range(4):
-
-            @pl.when(m == n)
+    def back_step(n, carry):
+        is_text = pick(n, [int(kind == "t") for kind, _ in STEPS])
+        arg = pick(n, [a for _, a in STEPS])
+        lax.fori_loop(pick(n, [0, 1]), pick(n, [1, 8]), soften, 0)
+
+        @pl.when(is_text == 1)
+        def _():
+            p = 7 - arg
+            cols = pl.ds(pl.multiple_of(p * 256, 256), 256)
+            res = dot3(Ph[:, cols], Pl[:, cols], Ih[...], Il[...], 0, 0)
+            Tb[2 * p] = res[:ROWS]
+            Tb[2 * p + 1] = res[ROWS:]
+
+        @pl.when(is_text == 0)
+        def _():
+            r = pl.ds(pl.multiple_of(arg * 256, 256), 256)
+            L[r, 0:E] = dot3(Ph[r, :], Pl[r, :], Th[...], Tl[...], 1, 0)
+
+        for m in range(len(STEPS)):
+
+            @pl.when(n == m)
             def _():
-                image_events(n)
+                for key in RETURN[m]:
+                    (image_send if key[0][0] == "I" else text_send)(key)
+                loss_send(m)
 
         return carry
 
-    lax.fori_loop(0, 4, image_step, 0)
-    second("A", 0)
-    second("B", 0)
-    add(iref(0), [w.wait(("ID", 1)), w.wait(("ID", -1))], ROWS, img_out, scale_ref[0])
+    lax.fori_loop(0, len(STEPS), back_step, 0)
     for d in (1, -1, 2):
         w.wait(("lz", d))
     loss_ref[...] = ((lbuf[10] + lbuf[11]) + (lbuf[12] + lbuf[13])) / (2.0 * 16384)

time: 184 us -> 139 us (0.76)
  Pallas kernels: 178 us -> 132 us
    pallas_call x1, Pallas kernels: 178 us -> 132 us  [on_device(): pl.pallas_call(kernel, out_shape=(jax.ShapeDtypeStruct((8, 128), F32), ja...]
where the time goes in v2:
time: 139 us; the launch traced here: 137 us
  Pallas kernels  132 us (95%)
  local copies, waits for them, and re-layouts  4.06 us (3%)
    pallas_call x1, Pallas kernels, on_device(): pl.pallas_call(kernel, out_shape=(jax.ShapeDtypeStruct((8, 128), F32), ja...  132 us
    unnamed x4, local copies, waits for them, and re-layouts  2.87 us

profile of v2, /device:TPU:1, one launch (start us, length us, event | category | flops | bytes accessed | tf_op | source)
XLA Modules:
  0.0 137.4 jit_solution(9323304498344050448)
XLA Ops:
  1.3 132.1 %contrastive.1 = (f32[8,128]{1,0:T(8,128)}, f32[128,1280]{1,0:T(8,128)}, f32[128,1280]{1,0:T(8,128)}) custom-call(f32[1]{0:T(128)} %bitcast.2.scale_ref, f32[128,1280]{1,0:T(8,128)} %img_ref.1, f32[128,1280]{1,0:T(8,128)} %txt_ref.1), custom_call_target="tpu_custom_call" | custom-call | tf_op jit(solution)/shard_map/contrastive/pallas_call | solution.py:550
  133.4 1.2 slice.3
  134.6 0.0 copy-start
  134.6 2.0 %copy.9 = f32[128,1280]{1,0:T(8,128)} copy(f32[128,1280]{1,0:T(8,128)} %get-tuple-element.13) | data formatting | bytes 1310720
  136.6 0.0 copy-done
  136.6 0.8 copy.10
Async XLA Ops:
  134.6 2.0 %copy-start = (f32[128,1280]{1,0:T(8,128)S(1)}, f32[128,1280]{1,0:T(8,128)}, u32[]{:S(2)}) copy-start(f32[128,1280]{1,0:T(8,128)} %get-tuple-element.14) | copy-start | bytes 1966084

commit v3 on v2

v3 whole, which is shorter than its diff:
```python
import functools

import jax
import jax.numpy as jnp
from jax import lax
from jax.experimental import pallas as pl
from jax.experimental.pallas import tpu as pltpu
from jax.sharding import PartitionSpec as P

MESH = pl.DeviceIdType.MESH
BF16, F32 = jnp.bfloat16, jnp.float32
LOG2E = 1.4426950408889634
LN2 = 0.6931471805599453

STEP = (0, 1, 3, 2)
ROWS = 128
HALF = ROWS // 2
E = 1280
IMG, TXT = 1024, 2048

TILES = ((0, 0), (1, 0), (0, 2), (1, 2), (2, 0), (2, 2), (0, 1), (1, 1), (2, 1), (3, 0), (3, 1), (3, 2), (0, 3), (1, 3), (2, 3), (3, 3))
GATHER = (
    (("TA", 0, 1), ("TB", 2, 0), ("IB", 2, 0), ("TB", 1, 0), ("IA", 0, 1), ("IB", 1, 0), ("S", 0, 0), ("TB", 0, 1),
     ("TA", 2, 0), ("IA", 2, 0), ("TA", 1, 0), ("IB", 0, 1), ("IA", 1, 0), ("TB", 2, 1), ("TA", 2, 1),
     ("IB", 3, 0, 0), ("TB", 3, 0, 1), ("IB", 1, 1), ("IA", 1, 1), ("TA", 1, 1), ("IA", 2, 1), ("S", 0, 1),
     ("S", 1, 0), ("S", 2, 0), ("TB", 3, 0, 0), ("TB", 1, 1), ("IB", 3, 0, 1), ("IB", 2, 1)),
    (("TA", 3, 0), ("IA", 3, 0), ("S", 2, 1), ("IA", 3, 1)),
    (("TB", 3, 1),),
    (("TA", 3, 1), ("IB", 3, 1)),
    (("S", 1, 1),),
    (),
    (("S", 3, 0),),
    (),
    (("S", 3, 1),),
    (),
    (),
    (),
    (),
    (),
    (),
    (),
    (),
)

STEPS = (("t", 4), ("t", 6), ("t", 7), ("i", 3), ("t", 3), ("t", 5), ("t", 2), ("i", 2), ("i", 1), ("t", 1), ("i", 0), ("t", 0))
RETURN = (
    (("S", 2, 0),),
    (("S", 3, 0),),
    (("S", 3, 1),),
    (("TA", "P", 0), ("IA", "P", 1), ("TA", "P", 1), ("IA", "P", 0), ("TB", "Y", 3), ("IB", "Y", 3)),
    (("S", 1, 1),),
    (("S", 2, 1),),
    (("TB", "Y", 1), ("S", 1, 0)),
    (("IB", "Y", 2), ("TA", "D", 0, 1), ("TA", "D", 1, -1), ("IB", "P", -1), ("IA", "D", 1, 1), ("TB", "Y", 2)),
    (("IA", "D", 1, -1), ("IB", "Y", 1), ("IA", "D", 0, 1), ("TB", "P", -1), ("TA", "D", 1, 1)),
    (("S", 0, 1),),
    (("IA", "D", 0, -1), ("IB", "Y", 0), ("TB", "Y", 0), ("TB", "D", -1), ("IB", "P", 1), ("TB", "P", 1)),
    (("S", 0, 0), ("IB", "D", -1), ("IA", "2"), ("TA", "2"), ("TA", "D", 0, -1), ("IB", "D", 1), ("TB", "D", 1),
     ("I", "F"), ("T", "F")),
)


def pick(n, values):
    return sum(jnp.where(n == j, v, 0) for j, v in enumerate(values))


def dot(a, b, ca, cb):
    return lax.dot_general(a, b, (((ca,), (cb,)), ((), ())), preferred_element_type=F32)


def dot3(ah, al, bh, bl, ca, cb):
    return dot(ah, bh, ca, cb) + (dot(ah, bl, ca, cb) + dot(al, bh, ca, cb))


class Wires:
    def __init__(self, send_sem, recv_sem):
        self.send_sem, self.recv_sem = send_sem, recv_sem
        self.sent, self.n_recv, self.arrivals = [], 0, {}

    def open(self, key, ref, *index):
        self.arrivals[key] = (ref, index, self.n_recv)
        self.n_recv += 1

    def send(self, src, key, dev):
        dst, index, n = self.arrivals[key]
        dst = dst.at[index]
        s = len(self.sent)
        cp = pltpu.make_async_remote_copy(
            src_ref=src,
            dst_ref=dst,
            send_sem=self.send_sem.at[s],
            recv_sem=self.recv_sem.at[n],
            device_id=dev,
            device_id_type=MESH,
        )
        cp.start()
        self.sent.append(dst.shape)

    def wait(self, key):
        dst, index, n = self.arrivals.pop(key)
        dst = dst.at[index]
        pltpu.make_async_copy(dst, dst, self.recv_sem.at[n]).wait()
        return dst

    def need(self, *keys):
        for key in keys:
            if key in self.arrivals:
                self.wait(key)

    def flush(self, like):
        for s, shape in enumerate(self.sent):
            ref = like(shape)
            pltpu.make_async_copy(ref, ref, self.send_sem.at[s]).wait()
        self.sent = []


def merge(parts):
    top = functools.reduce(jnp.maximum, [m for m, _ in parts])
    total = sum(s * jnp.exp2(m - top) for m, s in parts)
    return top, total


def kernel(
    scale_ref, img_ref, txt_ref,
    loss_ref, img_out, txt_out,
    Ib, Tb, Ih, Il, Th, Tl, L, Ph, Pl,
    row_m, row_s, col_m, col_s, rst, cst, acc, lbuf,
    iland, tland, eye,
    send_sem, recv_sem, local_sem,
):
    i, t = lax.axis_index("img"), lax.axis_index("txt")
    x, k = t // 2, t % 2
    z, y = i // 4, i % 4
    even = 1 - 2 * (y % 2)

    def dev(dx=0, dy=0, dz=0, dk=0):
        return (((z + dz) % 4) * 4 + (y + dy + 4) % 4, ((x + dx) % 4) * 2 + (k + dk) % 2)

    sib = dev(dk=1)
    xs = {1: dev(dx=1), -1: dev(dx=3), 2: dev(dx=2)}
    zs = {1: dev(dz=1), -1: dev(dz=3), 2: dev(dz=2)}
    yi, yt = dev(dy=even), dev(dy=-even)
    row_peers = [*xs.values(), yi, *(dev(dx=d, dy=even) for d in (1, 3, 2))]
    col_peers = [sib, yt, dev(dy=-even, dk=1)]
    peers = [*row_peers, *col_peers, *zs.values()]
    barrier = pltpu.get_barrier_semaphore()
    for peer in peers:
        pl.semaphore_signal(barrier, inc=1, device_id=peer, device_id_type=MESH)
    pl.semaphore_wait(barrier, len(peers))

    w = Wires(send_sem, recv_sem)

    def like(shape):
        if shape[-1] == E:
            return Ib.at[0, pl.ds(0, shape[0])]
        return {2: lbuf, 3: rst if shape[-2] == 8 else cst}[len(shape)].at[0]

    lo, hi = pl.ds(0, HALF), pl.ds(HALF, HALF)
    ring = {"I": xs, "T": zs}
    across = {"I": yi, "T": yt}
    own = {"I": img_ref, "T": txt_ref}

    def place(name, q, p):
        return (Ib, 2 * q + p) if name == "I" else (Tb, 4 * q + 2 * p)

    for name in "IT":
        for q in range(4):
            for p in range(2):
                if (q, p) == (0, 0):
                    continue
                w.open((name + "A", q, p), *place(name, q, p), lo)
                if (q, p) == (3, 0):
                    for n in range(2):
                        w.open((name + "B", 3, 0, n), *place(name, 3, 0), pl.ds(HALF + 32 * n, 32))
                else:
                    w.open((name + "B", q, p), *place(name, q, p), hi)
    for q in range(4):
        for p in range(2):
            w.open(("S", q, p), Tb, 4 * q + 2 * p + 1)

    def keys_of(name, q, p, parts="AB"):
        return [(name + part, q, p, *n) for part in parts for n in ((), (0,), (1,))]

    def block(name, q, p, rows):
        if (q, p) == (0, 0):
            return own[name].at[rows]
        ref, n = place(name, q, p)
        return ref.at[n, rows]

    def gather_send(key):
        if key[0] == "S":
            q, p = key[1:]
            w.need(*keys_of("T", q, p))
            w.send(block("T", q, p, pl.ds(0, ROWS)), key, sib)
            return
        name, part, q, p = key[0][0], key[0][1], key[1], key[2]
        rows = lo if part == "A" else hi
        if part == "A" and p == 1 and q == 0:
            source, dst = (0, 0), across[name]
        elif part == "B" and p == 1:
            source, dst = (q, 0), across[name]
        elif len(key) == 4:
            source, dst = (2 - key[3], 0), ring[name][1 - 2 * key[3]]
            rows = pl.ds(HALF + 32 * key[3], 32)
        elif q == 3:
            source, dst = (2 - p, p), ring[name][1 - 2 * p]
        else:
            source, dst = (0, p), ring[name][1 if q == 2 else -1]
        w.need(*keys_of(name, *source, part))
        w.send(block(name, *source, rows), key, dst)

    own_t = pltpu.make_async_copy(txt_ref, Tb.at[0], local_sem.at[0])
    own_i = pltpu.make_async_copy(img_ref, Ib.at[0], local_sem.at[1])
    for key in GATHER[0][:13]:
        gather_send(key)
    own_t.start()
    own_i.start()

    rows_iota = lax.broadcasted_iota(jnp.int32, (ROWS, ROWS), 0)
    cols_iota = lax.broadcasted_iota(jnp.int32, (ROWS, ROWS), 1)
    eye[...] = (rows_iota == cols_iota).astype(F32)
    row_m[...] = jnp.full((IMG, 128), -jnp.inf, F32)
    row_s[...] = jnp.zeros((IMG, 128), F32)
    col_m[...] = jnp.full((8, TXT), -jnp.inf, F32)
    col_s[...] = jnp.zeros((8, TXT), F32)

    def split_rows(src, first, count, high, low):
        def body(b, carry):
            n = first + b // 4
            o = pl.ds(pl.multiple_of(first * ROWS + b * 32, 32), 32)
            v = src[n, pl.ds(pl.multiple_of((b % 4) * 32, 32), 32), :]
            h = v.astype(BF16)
            high[o, :] = h
            low[o, :] = (v - h.astype(F32)).astype(BF16)
            return carry

        lax.fori_loop(0, 4 * count, body, 0)

    own_i.wait()
    own_t.wait()
    for key in GATHER[0][13:]:
        gather_send(key)

    s2 = scale_ref[0] * LOG2E
    seen_i = [int(qi not in [a for a, _ in TILES[:n]]) for n, (qi, _) in enumerate(TILES)]
    seen_t = [int(qt not in [b for _, b in TILES[:n]]) for n, (_, qt) in enumerate(TILES)]

    def tile(n, carry):
        for m, (qi, qt) in enumerate(TILES):

            @pl.when(n == m)
            def _():
                if m > 0:
                    for key in GATHER[m]:
                        gather_send(key)
                for p in range(2):
                    w.need(*keys_of("I", qi, p), *keys_of("T", qt, p), ("S", qt, p))

        a, b = pick(n, [qi for qi, _ in TILES]), pick(n, [qt for _, qt in TILES])

        @pl.when(pick(n, seen_i) == 1)
        def _():
            split_rows(Ib, 2 * a, 2, Ih, Il)

        @pl.when(pick(n, seen_t) == 1)
        def _():
            split_rows(Tb, 4 * b, 4, Th, Tl)

        rows = pl.ds(pl.multiple_of(a * 256, 256), 256)
        cols = pl.ds(pl.multiple_of(b * 512, 512), 512)
        L[rows, cols] = s2 * dot3(Ih[rows, :], Il[rows, :], Th[cols, :], Tl[cols, :], 1, 1)

        def peak(c, top):
            r = pl.ds(pl.multiple_of(a * 256 + c * ROWS, ROWS), ROWS)
            v = L[r, cols]
            vs = [v[:, 128 * j : 128 * j + 128] for j in range(4)]
            old = row_m[r, :]
            new = functools.reduce(jnp.maximum, vs, old)
            row_s[r, :] = row_s[r, :] * jnp.exp2(old - new) + sum(jnp.exp2(u - new) for u in vs)
            row_m[r, :] = new
            return jnp.maximum(top, jnp.max(v.reshape(ROWS // 8, 8, 512), axis=0))

        old = col_m[:, cols]
        top = lax.fori_loop(0, 2, peak, old)

        def total(c, s):
            r = pl.ds(pl.multiple_of(a * 256 + c * ROWS, ROWS), ROWS)
            v = L[r, cols].reshape(ROWS // 8, 8, 512)
            return s + jnp.sum(jnp.exp2(v - top[None]), axis=0)

        col_s[:, cols] = lax.fori_loop(0, 2, total, col_s[:, cols] * jnp.exp2(old - top))
        col_m[:, cols] = top
        return carry

    lax.fori_loop(0, len(TILES), tile, 0)

    def step_of(q):
        return q + q // 2 - 2 * (q // 3)

    def img_block(s):
        return ((x + step_of(s // 2)) % 4) * 2 + (y + s % 2) % 2

    def txt_block(s):
        return (((z + step_of(s // 4)) % 4) * 2 + (y + (s // 2) % 2) % 2) * 2 + (k + s % 2) % 2

    def fold_cols(s, carry):
        c = pl.ds(pl.multiple_of(s * ROWS, ROWS), ROWS)
        m8 = col_m[:, c]
        m1 = jnp.max(m8, axis=0, keepdims=True)
        at = pl.ds(txt_block(s), 1)
        cst[0, 0, at, :] = m1
        cst[0, 1, at, :] = jnp.sum(col_s[:, c] * jnp.exp2(m8 - m1), axis=0, keepdims=True)
        return carry

    def fold_rows(s, carry):
        r = pl.ds(pl.multiple_of(s * ROWS, ROWS), ROWS)
        mt, st = row_m[r, :].T, row_s[r, :].T
        m1 = jnp.max(mt, axis=0, keepdims=True)
        at = pl.ds(img_block(s), 1)
        rst[0, 0, at, :] = m1
        rst[0, 1, at, :] = jnp.sum(st * jnp.exp2(mt - m1), axis=0, keepdims=True)
        return carry

    lax.fori_loop(0, 16, fold_cols, 0)
    w.flush(like)
    assert not w.arrivals
    for n in range(7):
        w.open(("r", n), rst, 1 + n)
    for n in range(3):
        w.open(("c1", n), cst, 1 + n)
        w.open(("c2", n), cst, 5 + n)
    for n in range(3):
        w.send(cst.at[0], ("c1", n), col_peers[n])
    lax.fori_loop(0, 8, fold_rows, 0)
    for n in range(7):
        w.send(rst.at[0], ("r", n), row_peers[n])
    for n in range(3):
        w.wait(("c1", n))
    cst[4, 0], cst[4, 1] = merge([(cst[n, 0], cst[n, 1]) for n in range(4)])
    for n, d in enumerate((1, -1, 2)):
        w.send(cst.at[4], ("c2", n), zs[d])
    for n in range(7):
        w.wait(("r", n))
    m, s = merge([(rst[n, 0], rst[n, 1]) for n in range(8)])
    row_lse = m + jnp.log2(s)
    rst[8, 0] = row_lse + 1.0

    def spread(s, carry):
        r = pl.ds(pl.multiple_of(s * ROWS, ROWS), ROWS)
        v = rst[8, 0, pl.ds(img_block(s), 1), :]
        row_m[r, :] = jnp.broadcast_to(v, (ROWS, 128)).T
        return carry

    lax.fori_loop(0, 8, spread, 0)
    for n in range(3):
        w.wait(("c2", n))
    m, s = merge([(cst[n, 0], cst[n, 1]) for n in range(4, 8)])
    col_lse = m + jnp.log2(s)
    w.flush(like)
    cst[8, 0] = col_lse + 1.0
    acc[...] = jnp.full((8, 128), LN2 * (jnp.sum(row_lse) / 8 + jnp.sum(col_lse) / 16), F32)

    for name, land in (("I", iland), ("T", tland)):
        for p in range(2):
            w.open((name + "A", "P", p), land, p)
            for n, d in enumerate((1, -1)):
                w.open((name + "A", "D", p, d), land, 2 + 2 * p + n)
        w.open((name + "A", "2"), land, 6)
        for q in range(4):
            w.open((name + "B", "Y", q), land, 7 + q)
        for n, d in enumerate((1, -1)):
            w.open((name + "B", "P", d), land, 11, pl.ds(32 * n, 32))
            w.open((name + "B", "D", d), land, 12 + n)
    for q in range(4):
        for p in range(2):
            w.open(("S", q, p), Ib, 2 * q + p)
    for n in range(7):
        w.open(("l1", n), lbuf, 1 + n)
    for n in range(3):
        w.open(("l2", n), lbuf, 9 + n)
        w.open(("l3", n), lbuf, 13 + n)

    def add(dst, srcs, rows, out=None):
        step = 16

        def body(b, carry):
            r = pl.ds(pl.multiple_of(b * step, step), step)
            v = dst[r, :]
            for src in srcs:
                v = v + src[r, :]
            (dst if out is None else out)[r, :] = v
            return carry

        lax.fori_loop(0, rows // step, body, 0)

    summed = set()

    def sums(name, q, p, at, rows):
        if name == "I":
            return L.at[pl.ds((2 * q + p) * ROWS + at, rows), pl.ds(0, E)]
        if (q, p) not in summed:
            summed.add((q, p))
            add(Tb.at[4 * q + 2 * p], [w.wait(("S", q, p))], ROWS)
        return Tb.at[4 * q + 2 * p, pl.ds(at, rows)]

    def back_send(key):
        if key[0] == "S":
            q, p = key[1:]
            w.send(Tb.at[4 * q + 2 * p + 1], key, sib)
            return
        name, kind = key[0][0], key[1]
        way, part = ring[name], key[0]
        if part == name:
            out = img_out if name == "I" else txt_out
            A, B = name + "A", name + "B"
            srcs = [w.wait((A, "D", 0, 1)), w.wait((A, "D", 0, -1)), w.wait((A, "2"))]
            add(sums(name, 0, 0, 0, HALF), srcs, HALF, out.at[lo])
            srcs = [w.wait((B, "Y", 0)), w.wait((B, "D", 1)), w.wait((B, "D", -1))]
            add(sums(name, 0, 0, HALF, HALF), srcs, HALF, out.at[hi])
        elif part[1] == "A":
            if kind == "P":
                w.send(sums(name, 3, key[2], 0, HALF), key, way[2 * key[2] - 1])
            elif kind == "D":
                p, d = key[2:]
                mine = sums(name, 2 if d == 1 else 1, p, 0, HALF)
                if p == (1 - d) // 2:
                    add(mine, [w.wait((part, "P", p))], HALF)
                w.send(mine, key, way[-d])
            else:
                mine = sums(name, 0, 1, 0, HALF)
                add(mine, [w.wait((part, "D", 1, 1)), w.wait((part, "D", 1, -1))], HALF)
                w.send(mine, key, across[name])
        elif kind == "Y":
            w.send(sums(name, key[2], 1, HALF, HALF), key, across[name])
        elif kind == "P":
            d = key[2]
            if (name, "far") not in summed:
                summed.add((name, "far"))
                add(sums(name, 3, 0, HALF, HALF), [w.wait((part, "Y", 3))], HALF)
            w.send(sums(name, 3, 0, HALF if d == 1 else HALF + 32, 32), key, way[-d])
        else:
            d = key[2]
            q = 2 if d == 1 else 1
            mine = sums(name, q, 0, HALF, HALF)
            add(mine, [w.wait((part, "Y", q))], HALF)
            add(mine.at[pl.ds(0 if d == 1 else 32, 32)], [w.wait((part, "P", d))], 32)
            w.send(mine, key, way[-d])

    lbuf[0] = jnp.zeros((8, 128), F32)

    def soften(n, carry):
        first = STEPS[0][1]
        p = pick(n, [first] + [m for m in range(8) if m != first])
        cols = pl.ds(pl.multiple_of(p * 256, 256), 256)
        cl = jnp.concatenate([cst[8, 0, pl.ds(txt_block(2 * p + j), 1), :] for j in range(2)], axis=1)

        def soft(b, inner):
            r = pl.ds(pl.multiple_of(b * ROWS, ROWS), ROWS)
            v = L[r, cols]
            rl = row_m[r, :]
            g = jnp.exp2(v - jnp.concatenate([rl, rl], axis=1)) + jnp.exp2(v - cl)
            h = g.astype(BF16)
            Ph[r, cols] = h
            Pl[r, cols] = (g - h.astype(F32)).astype(BF16)
            return inner

        lax.fori_loop(0, IMG // ROWS, soft, 0)
        for j in range(2):
            s = 2 * p + j
            owner = (x * 2 + (k + j) % 2) * 16 + ((z + step_of(s // 4)) % 4) * 4
            owner = owner + (y + ((s // 2) % 2) * (4 - even)) % 4
            bi, bt = owner // 8, owner % 8

            @pl.when((bi // 4 == z) & ((bi % 4) // 2 == y // 2) & (bt % 2 == k))
            def _():
                u = step_of((bt // 2 + 4 - x) % 4) * 2 + (bi + y) % 2
                r = pl.ds(pl.multiple_of(u * ROWS, ROWS), ROWS)
                c = pl.ds(pl.multiple_of(s * ROWS, ROWS), ROWS)
                v = L[r, c]
                g = jnp.exp2(v - row_m[r, :]) + jnp.exp2(v - cl[:, 128 * j : 128 * j + 128]) - eye[...]
                h = g.astype(BF16)
                Ph[r, c] = h
                Pl[r, c] = (g - h.astype(F32)).astype(BF16)
                lbuf[0] += jnp.sum((v * eye[...]).reshape(ROWS // 8, 8, 128), axis=0)

        return carry

    def loss_send(m):
        if m == 1:
            total = jnp.sum(acc[...]) / 1024 - 2.0 * LN2 * jnp.sum(lbuf[0])
            lbuf[0] = jnp.full((8, 128), total, F32)
            for n in range(7):
                w.send(lbuf.at[0], ("l1", n), row_peers[n])
        if m == 4:
            for n in range(7):
                w.wait(("l1", n))
            lbuf[8] = sum(lbuf[n] for n in range(8))
            for n in range(3):
                w.send(lbuf.at[8], ("l2", n), col_peers[n])
        if m == 7:
            for n in range(3):
                w.wait(("l2", n))
            lbuf[12] = sum(lbuf[n] for n in range(8, 12))
            for n, d in enumerate((1, -1, 2)):
                w.send(lbuf.at[12], ("l3", n), zs[d])

    def back_step(n, carry):
        is_text = pick(n, [int(kind == "t") for kind, _ in STEPS])
        arg = pick(n, [a for _, a in STEPS])
        lax.fori_loop(pick(n, [0, 1]), pick(n, [1, 8]), soften, 0)

        @pl.when(is_text == 1)
        def _():
            cols = pl.ds(pl.multiple_of(arg * 256, 256), 256)
            res = dot3(Ph[:, cols], Pl[:, cols], Ih[...], Il[...], 0, 0)
            Tb[2 * arg] = res[:ROWS]
            Tb[2 * arg + 1] = res[ROWS:]

        @pl.when(is_text == 0)
        def _():
            r = pl.ds(pl.multiple_of(arg * 256, 256), 256)
            L[r, 0:E] = dot3(Ph[r, :], Pl[r, :], Th[...], Tl[...], 1, 0)

        for m in range(len(STEPS)):

            @pl.when(n == m)
            def _():
                for key in RETURN[m]:
                    back_send(key)
                loss_send(m)

        return carry

    lax.fori_loop(0, len(STEPS), back_step, 0)
    for n in range(3):
        w.wait(("l3", n))
    loss_ref[0] = jnp.sum(sum(lbuf[n] for n in range(12, 16))) / (1024 * 2.0 * 16384)
    w.flush(like)
    assert not w.arrivals


def on_device(image_emb, text_emb, logit_scale):
    vm = pltpu.VMEM
    loss, image_grad, text_grad = pl.pallas_call(
        kernel,
        out_shape=(
            jax.ShapeDtypeStruct((1,), F32),
            jax.ShapeDtypeStruct((ROWS, E), F32),
            jax.ShapeDtypeStruct((ROWS, E), F32),
        ),
        in_specs=[
            pl.BlockSpec(memory_space=pltpu.SMEM),
            pl.BlockSpec(memory_space=pl.ANY),
            pl.BlockSpec(memory_space=pl.ANY),
        ],
        out_specs=[pl.BlockSpec(memory_space=pltpu.SMEM)] + [pl.BlockSpec(memory_space=vm)] * 2,
        scratch_shapes=[
            vm((8, ROWS, E), F32),
            vm((16, ROWS, E), F32),
            vm((IMG, E), BF16),
            vm((IMG, E), BF16),
            vm((TXT, E), BF16),
            vm((TXT, E), BF16),
            vm((IMG, TXT), F32),
            vm((IMG, TXT), BF16),
            vm((IMG, TXT), BF16),
            vm((IMG, 128), F32),
            vm((IMG, 128), F32),
            vm((8, TXT), F32),
            vm((8, TXT), F32),
            vm((9, 2, 8, 128), F32),
            vm((9, 2, 16, 128), F32),
            vm((8, 128), F32),
            vm((16, 8, 128), F32),
            vm((14, HALF, E), F32),
            vm((14, HALF, E), F32),
            vm((ROWS, ROWS), F32),
            pltpu.SemaphoreType.DMA((56,)),
            pltpu.SemaphoreType.DMA((112,)),
            pltpu.SemaphoreType.DMA((2,)),
        ],
        compiler_params=pltpu.CompilerParams(
            collective_id=0, has_side_effects=True, vmem_limit_bytes=63 * 2**20
        ),
        name="contrastive",
    )(logit_scale.reshape(1), image_emb, text_emb)
    return loss.reshape(()), logit_scale * image_grad, logit_scale * text_grad


def solution(mesh):
    in_specs = (P(("img", "txt"), None), P(("txt", "img"), None), P())
    out_specs = (P(), P(("img", "txt"), None), P(("txt", "img"), None))
    return jax.shard_map(
        on_device, mesh=mesh, in_specs=in_specs, out_specs=out_specs, check_vma=False
    )
```

time: 139 us -> 131 us (0.942); the launches traced: 137 us -> 131 us
  Pallas kernels: 132 us -> 125 us
  local copies, waits for them, and re-layouts: 4.06 us -> 0 us
  other arithmetic: 0 us -> 2.43 us
  between operations: 1.29 us -> 3.09 us
    pallas_call x1, Pallas kernels: 132 us -> 125 us  [on_device(): pl.pallas_call(kernel, out_shape=(jax.ShapeDtypeStruct((1,), F32), jax.Sh...]
    unnamed x4 -> x0, local copies, waits for them, and re-layouts: 2.87 us -> none
    mul x0 -> x1, other arithmetic: none -> 2.43 us  [on_device(): return (loss.reshape(()), logit_scale * image_grad, logit_scale * text_grad)]
where the time goes in v3:
time: 131 us
  Pallas kernels  125 us (95%)
  between operations  3.09 us (2%)
  other arithmetic  2.43 us (2%)
    pallas_call x1, Pallas kernels, on_device(): pl.pallas_call(kernel, out_shape=(jax.ShapeDtypeStruct((1,), F32), jax.Sh...  125 us

profile of v3, /device:TPU:1, one launch (start us, length us, event | category | flops | bytes accessed | tf_op | source)
XLA Modules:
  0.0 130.9 jit_solution(2954107031359135434)
XLA Ops:
  1.3 125.4 %contrastive.1 = (f32[1]{0:T(128)}, f32[128,1280]{1,0:T(8,128)}, f32[128,1280]{1,0:T(8,128)}) custom-call(f32[1]{0:T(128)} %bitcast.2.scale_ref, f32[128,1280]{1,0:T(8,128)} %img_ref.1, f32[128,1280]{1,0:T(8,128)} %txt_ref.1), custom_call_target="tpu_custom_call" | custom-call | tf_op jit(solution)/shard_map/contrastive/pallas_call | solution.py:544
  126.7 2.4 %broadcast_multiply_fusion = (f32[128,1280]{1,0:T(8,128)}, f32[128,1280]{1,0:T(8,128)}) fusion(f32[128,1280]{1,0:T(8,128)} %get-tuple-element.8, f32[]{:T(128)} %copy.7, f32[128,1280]{1,0:T(8,128)} %get-tuple-element.7), kind=kLoop, calls=%fused_computation | loop fusion | flops 327680 | bytes 2621444 | tf_op jit(solution)/shard_map/mul | solution.py:587

commit v4 on v3

--- a/solution.py
+++ b/solution.py
@@ -13,6 +13,7 @@
 LN2 = 0.6931471805599453
 
 STEP = (0, 1, 3, 2)
+F8 = jnp.float8_e4m3fn
 ROWS = 128
 HALF = ROWS // 2
 E = 1280
@@ -42,20 +43,20 @@
     (),
 )
 
-STEPS = (("t", 4), ("t", 6), ("t", 7), ("i", 3), ("t", 3), ("t", 5), ("t", 2), ("i", 2), ("i", 1), ("t", 1), ("i", 0), ("t", 0))
+STEPS = (("t", 7), ("t", 6), ("i", 3), ("t", 5), ("t", 3), ("i", 2), ("t", 4), ("i", 1), ("t", 1), ("t", 2), ("i", 0), ("t", 0))
 RETURN = (
-    (("S", 2, 0),),
-    (("S", 3, 0),),
     (("S", 3, 1),),
-    (("TA", "P", 0), ("IA", "P", 1), ("TA", "P", 1), ("IA", "P", 0), ("TB", "Y", 3), ("IB", "Y", 3)),
+    (("S", 3, 0), ("TB", "Y", 3), ("TA", "P", 1)),
+    (("IA", "P", 0), ("IA", "P", 1), ("IB", "Y", 3), ("TA", "P", 0)),
+    (("S", 2, 1),),
     (("S", 1, 1),),
-    (("S", 2, 1),),
-    (("TB", "Y", 1), ("S", 1, 0)),
-    (("IB", "Y", 2), ("TA", "D", 0, 1), ("TA", "D", 1, -1), ("IB", "P", -1), ("IA", "D", 1, 1), ("TB", "Y", 2)),
-    (("IA", "D", 1, -1), ("IB", "Y", 1), ("IA", "D", 0, 1), ("TB", "P", -1), ("TA", "D", 1, 1)),
+    (("IB", "Y", 2), ("IA", "D", 1, 1), ("TB", "P", -1), ("TA", "D", 1, 1), ("TB", "Y", 2), ("TA", "D", 1, -1)),
+    (("IB", "P", -1), ("S", 2, 0)),
+    (("IA", "D", 1, -1), ("IB", "Y", 1), ("IA", "D", 0, 1), ("TA", "D", 0, 1), ("TB", "Y", 1)),
     (("S", 0, 1),),
-    (("IA", "D", 0, -1), ("IB", "Y", 0), ("TB", "Y", 0), ("TB", "D", -1), ("IB", "P", 1), ("TB", "P", 1)),
-    (("S", 0, 0), ("IB", "D", -1), ("IA", "2"), ("TA", "2"), ("TA", "D", 0, -1), ("IB", "D", 1), ("TB", "D", 1),
+    (("S", 1, 0), ("IA", "D", 0, -1)),
+    (("IB", "Y", 0), ("TB", "Y", 0), ("IB", "P", 1), ("TA", "D", 0, -1), ("TB", "P", 1)),
+    (("S", 0, 0), ("IB", "D", -1), ("IA", "2"), ("TA", "2"), ("TB", "D", -1), ("IB", "D", 1), ("TB", "D", 1),
      ("I", "F"), ("T", "F")),
 )
 
@@ -123,7 +124,8 @@
 def kernel(
     scale_ref, img_ref, txt_ref,
     loss_ref, img_out, txt_out,
-    Ib, Tb, Ih, Il, Th, Tl, L, Ph, Pl,
+    Ib, Tb, Ih, Il, Th, Tl, L,
+    P8h, P8l, I8h, I8l, T8h, T8l,
     row_m, row_s, col_m, col_s, rst, cst, acc, lbuf,
     iland, tland, eye,
     send_sem, recv_sem, local_sem,
@@ -334,11 +336,32 @@
     lax.fori_loop(0, 8, fold_rows, 0)
     for n in range(7):
         w.send(rst.at[0], ("r", n), row_peers[n])
+    def largest(src, count):
+        def body(b, top):
+            v = jnp.abs(src[pl.ds(pl.multiple_of(b * 64, 64), 64), :]).astype(F32)
+            return jnp.maximum(top, jnp.max(v.reshape(8, 8, E), axis=0))
+
+        return jnp.max(lax.fori_loop(0, count // 64, body, jnp.zeros((8, E), F32)))
+
+    i_scale = 240.0 / jnp.maximum(largest(Ih, IMG), 1e-30)
+    t_scale = 240.0 / jnp.maximum(largest(Th, TXT), 1e-30)
+
+    def to_eight(high, low, count, scale, high8, low8):
+        def body(b, carry):
+            r = pl.ds(pl.multiple_of(b * 64, 64), 64)
+            high8[r, :] = (high[r, :].astype(F32) * scale).astype(F8)
+            low8[r, :] = (low[r, :].astype(F32) * (256.0 * scale)).astype(F8)
+            return carry
+
+        lax.fori_loop(0, count // 64, body, 0)
+
     for n in range(3):
         w.wait(("c1", n))
     cst[4, 0], cst[4, 1] = merge([(cst[n, 0], cst[n, 1]) for n in range(4)])
     for n, d in enumerate((1, -1, 2)):
         w.send(cst.at[4], ("c2", n), zs[d])
+    to_eight(Ih, Il, IMG, i_scale, I8h, I8l)
+    to_eight(Th, Tl, TXT, t_scale, T8h, T8l)
     for n in range(7):
         w.wait(("r", n))
     m, s = merge([(rst[n, 0], rst[n, 1]) for n in range(8)])
@@ -448,6 +471,17 @@
 
     lbuf[0] = jnp.zeros((8, 128), F32)
 
+    def put_grad(g, r, c, width):
+        first, size = r
+        h = g.astype(BF16)
+        rows = pl.ds(pl.multiple_of(first, ROWS), size)
+        cols = pl.ds(pl.multiple_of(c, ROWS), width)
+        below = pl.ds(pl.multiple_of(first + (c // IMG) * IMG, ROWS), size)
+        Tl[below, pl.ds(pl.multiple_of(c % IMG, ROWS), width)] = h
+        hf = h.astype(F32)
+        P8h[rows, cols] = (hf * 256.0).astype(F8)
+        P8l[rows, cols] = ((g - hf) * 65536.0).astype(F8)
+
     def soften(n, carry):
         first = STEPS[0][1]
         p = pick(n, [first] + [m for m in range(8) if m != first])
@@ -459,9 +493,7 @@
             v = L[r, cols]
             rl = row_m[r, :]
             g = jnp.exp2(v - jnp.concatenate([rl, rl], axis=1)) + jnp.exp2(v - cl)
-            h = g.astype(BF16)
-            Ph[r, cols] = h
-            Pl[r, cols] = (g - h.astype(F32)).astype(BF16)
+            put_grad(g, (b * ROWS, ROWS), p * 256, 256)
             return inner
 
         lax.fori_loop(0, IMG // ROWS, soft, 0)
@@ -478,9 +510,7 @@
                 c = pl.ds(pl.multiple_of(s * ROWS, ROWS), ROWS)
                 v = L[r, c]
                 g = jnp.exp2(v - row_m[r, :]) + jnp.exp2(v - cl[:, 128 * j : 128 * j + 128]) - eye[...]
-                h = g.astype(BF16)
-                Ph[r, c] = h
-                Pl[r, c] = (g - h.astype(F32)).astype(BF16)
+                put_grad(g, (u * ROWS, ROWS), s * ROWS, ROWS)
                 lbuf[0] += jnp.sum((v * eye[...]).reshape(ROWS // 8, 8, 128), axis=0)
 
         return carry
@@ -512,14 +542,20 @@
         @pl.when(is_text == 1)
         def _():
             cols = pl.ds(pl.multiple_of(arg * 256, 256), 256)
-            res = dot3(Ph[:, cols], Pl[:, cols], Ih[...], Il[...], 0, 0)
+            below = pl.ds(pl.multiple_of((arg // 4) * IMG, IMG), IMG)
+            high = dot(Tl[below, pl.ds(pl.multiple_of((arg % 4) * 256, 256), 256)], Ih[...], 0, 0)
+            cross = dot(P8h[:, cols], I8l[...], 0, 0) + dot(P8l[:, cols], I8h[...], 0, 0)
+            res = high + (1.0 / (65536.0 * i_scale)) * cross
             Tb[2 * arg] = res[:ROWS]
             Tb[2 * arg + 1] = res[ROWS:]
 
         @pl.when(is_text == 0)
         def _():
             r = pl.ds(pl.multiple_of(arg * 256, 256), 256)
-            L[r, 0:E] = dot3(Ph[r, :], Pl[r, :], Th[...], Tl[...], 1, 0)
+            r2 = pl.ds(pl.multiple_of(IMG + arg * 256, 256), 256)
+            high = dot(Tl[r, 0:IMG], Th[0:IMG, :], 1, 0) + dot(Tl[r2, 0:IMG], Th[IMG:TXT, :], 1, 0)
+            cross = dot(P8h[r, :], T8l[...], 1, 0) + dot(P8l[r, :], T8h[...], 1, 0)
+            L[r, 0:E] = high + (1.0 / (65536.0 * t_scale)) * cross
 
         for m in range(len(STEPS)):
 
@@ -562,8 +598,12 @@
             vm((TXT, E), BF16),
             vm((TXT, E), BF16),
             vm((IMG, TXT), F32),
-            vm((IMG, TXT), BF16),
-            vm((IMG, TXT), BF16),
+            vm((IMG, TXT), F8),
+            vm((IMG, TXT), F8),
+            vm((IMG, E), F8),
+            vm((IMG, E), F8),
+            vm((TXT, E), F8),
+            vm((TXT, E), F8),
             vm((IMG, 128), F32),
             vm((IMG, 128), F32),
             vm((8, TXT), F32),

time: 131 us -> 125 us (0.954)
  Pallas kernels: 125 us -> 119 us
    pallas_call x1, Pallas kernels: 125 us -> 119 us  [on_device(): pl.pallas_call(kernel, out_shape=(jax.ShapeDtypeStruct((1,), F32), jax.Sh...]
where the time goes in v4:
time: 125 us
  Pallas kernels  119 us (95%)
  between operations  3.09 us (2%)
  other arithmetic  2.43 us (2%)
    pallas_call x1, Pallas kernels, on_device(): pl.pallas_call(kernel, out_shape=(jax.ShapeDtypeStruct((1,), F32), jax.Sh...  119 us

profile of v4, /device:TPU:1, one launch (start us, length us, event | category | flops | bytes accessed | tf_op | source)
XLA Modules:
  0.0 124.5 jit_solution(10384753711370275292)
XLA Ops:
  1.3 119.0 %contrastive.1 = (f32[1]{0:T(128)}, f32[128,1280]{1,0:T(8,128)}, f32[128,1280]{1,0:T(8,128)}) custom-call(f32[1]{0:T(128)} %bitcast.2.scale_ref, f32[128,1280]{1,0:T(8,128)} %img_ref.1, f32[128,1280]{1,0:T(8,128)} %txt_ref.1), custom_call_target="tpu_custom_call" | custom-call | tf_op jit(solution)/shard_map/contrastive/pallas_call | solution.py:580
  120.3 2.4 %broadcast_multiply_fusion = (f32[128,1280]{1,0:T(8,128)}, f32[128,1280]{1,0:T(8,128)}) fusion(f32[128,1280]{1,0:T(8,128)} %get-tuple-element.8, f32[]{:T(128)} %copy.7, f32[128,1280]{1,0:T(8,128)} %get-tuple-element.7), kind=kLoop, calls=%fused_computation | loop fusion | flops 327680 | bytes 2621444 | tf_op jit(solution)/shard_map/mul | solution.py:627

commit v5 on v4

--- a/solution.py
+++ b/solution.py
@@ -17,6 +17,7 @@
 ROWS = 128
 HALF = ROWS // 2
 E = 1280
+CHUNK = 64
 IMG, TXT = 1024, 2048
 
 TILES = ((0, 0), (1, 0), (0, 2), (1, 2), (2, 0), (2, 2), (0, 1), (1, 1), (2, 1), (3, 0), (3, 1), (3, 2), (0, 3), (1, 3), (2, 3), (3, 3))
@@ -43,22 +44,30 @@
     (),
 )
 
-STEPS = (("t", 7), ("t", 6), ("i", 3), ("t", 5), ("t", 3), ("i", 2), ("t", 4), ("i", 1), ("t", 1), ("t", 2), ("i", 0), ("t", 0))
+STEPS = (("t", 7), ("t", 6), ("i", 7), ("t", 5), ("i", 5), ("t", 3), ("t", 4), ("i", 6), ("i", 3), ("t", 1), ("t", 2), ("i", 2), ("i", 1), ("i", 4), ("t", 0), ("i", 0))
 RETURN = (
     (("S", 3, 1),),
-    (("S", 3, 0), ("TB", "Y", 3), ("TA", "P", 1)),
-    (("IA", "P", 0), ("IA", "P", 1), ("IB", "Y", 3), ("TA", "P", 0)),
+    (("S", 3, 0),),
+    (("TB", "Y", 3), ("IB", "Y", 3), ("TA", "P", 1), ("IA", "P", 1), ("TA", "P", 0)),
     (("S", 2, 1),),
-    (("S", 1, 1),),
-    (("IB", "Y", 2), ("IA", "D", 1, 1), ("TB", "P", -1), ("TA", "D", 1, 1), ("TB", "Y", 2), ("TA", "D", 1, -1)),
-    (("IB", "P", -1), ("S", 2, 0)),
-    (("IA", "D", 1, -1), ("IB", "Y", 1), ("IA", "D", 0, 1), ("TA", "D", 0, 1), ("TB", "Y", 1)),
-    (("S", 0, 1),),
-    (("S", 1, 0), ("IA", "D", 0, -1)),
-    (("IB", "Y", 0), ("TB", "Y", 0), ("IB", "P", 1), ("TA", "D", 0, -1), ("TB", "P", 1)),
-    (("S", 0, 0), ("IB", "D", -1), ("IA", "2"), ("TA", "2"), ("TB", "D", -1), ("IB", "D", 1), ("TB", "D", 1),
-     ("I", "F"), ("T", "F")),
+    (("IA", "D", 1, 1),),
+    (("S", 1, 1), ("TB", "Y", 2), ("IB", "Y", 2)),
+    (("S", 2, 0), ("TA", "D", 1, 1)),
+    (("IB", "P", -1), ("TA", "D", 1, -1), ("IA", "P", 0)),
+    (),
+    (("S", 0, 1), ("IA", "D", 1, -1), ("TB", "Y", 1), ("TA", "D", 0, 1), ("IB", "Y", 1)),
+    (("S", 1, 0), ("TB", "P", -1)),
+    (("IB", "P", 1),),
+    (("IA", "D", 0, -1), ("TA", "2"), ("TA", "D", 0, -1), ("IB", "Y", 0)),
+    (("IA", "D", 0, 1), ("TB", "P", 1)),
+    (("S", 0, 0),),
+    (("IB", "D", -1), ("TB", "D", -1), ("IA", "2"), ("TB", "Y", 0), ("TB", "D", 1), ("IB", "D", 1), ("T", "F"),
+     ("I", "F")),
 )
+
+
+FIRST_IMAGE = [kind for kind, _ in STEPS].index("i")
+SOFT = [n if n <= FIRST_IMAGE else 8 for n in range(len(STEPS) + 1)]
 
 
 def pick(n, values):
@@ -247,6 +256,35 @@
     seen_i = [int(qi not in [a for a, _ in TILES[:n]]) for n, (qi, _) in enumerate(TILES)]
     seen_t = [int(qt not in [b for _, b in TILES[:n]]) for n, (_, qt) in enumerate(TILES)]
 
+    def tile_at(n):
+        return pick(n, [qi for qi, _ in TILES]), pick(n, [qt for _, qt in TILES])
+
+    def logits(a, b):
+        rows = pl.ds(pl.multiple_of(a * 256, 256), 256)
+        cols = pl.ds(pl.multiple_of(b * 512, 512), 512)
+        L[rows, cols] = s2 * dot3(Ih[rows, :], Il[rows, :], Th[cols, :], Tl[cols, :], 1, 1)
+
+    def statistics(n):
+        a, b = tile_at(n)
+        cols = pl.ds(pl.multiple_of(b * 512, 512), 512)
+        old = col_m[:, cols]
+        top = old
+        some = [pl.ds(pl.multiple_of(a * 256 + CHUNK * c, CHUNK), CHUNK) for c in range(256 // CHUNK)]
+        for r in some:
+            v = L[r, cols]
+            vs = [v[:, 128 * j : 128 * j + 128] for j in range(4)]
+            was = row_m[r, :]
+            new = functools.reduce(jnp.maximum, vs, was)
+            row_s[r, :] = row_s[r, :] * jnp.exp2(was - new) + sum(jnp.exp2(u - new) for u in vs)
+            row_m[r, :] = new
+            top = jnp.maximum(top, jnp.max(v.reshape(CHUNK // 8, 8, 512), axis=0))
+        total = col_s[:, cols] * jnp.exp2(old - top)
+        for r in some:
+            v = L[r, cols].reshape(CHUNK // 8, 8, 512)
+            total = total + jnp.sum(jnp.exp2(v - top[None]), axis=0)
+        col_s[:, cols] = total
+        col_m[:, cols] = top
+
     def tile(n, carry):
         for m, (qi, qt) in enumerate(TILES):
 
@@ -258,7 +296,7 @@
                 for p in range(2):
                     w.need(*keys_of("I", qi, p), *keys_of("T", qt, p), ("S", qt, p))
 
-        a, b = pick(n, [qi for qi, _ in TILES]), pick(n, [qt for _, qt in TILES])
+        a, b = tile_at(n)
 
         @pl.when(pick(n, seen_i) == 1)
         def _():
@@ -268,33 +306,19 @@
         def _():
             split_rows(Tb, 4 * b, 4, Th, Tl)
 
-        rows = pl.ds(pl.multiple_of(a * 256, 256), 256)
-        cols = pl.ds(pl.multiple_of(b * 512, 512), 512)
-        L[rows, cols] = s2 * dot3(Ih[rows, :], Il[rows, :], Th[cols, :], Tl[cols, :], 1, 1)
-
-        def peak(c, top):
-            r = pl.ds(pl.multiple_of(a * 256 + c * ROWS, ROWS), ROWS)
-            v = L[r, cols]
-            vs = [v[:, 128 * j : 128 * j + 128] for j in range(4)]
-            old = row_m[r, :]
-            new = functools.reduce(jnp.maximum, vs, old)
-            row_s[r, :] = row_s[r, :] * jnp.exp2(old - new) + sum(jnp.exp2(u - new) for u in vs)
-            row_m[r, :] = new
-            return jnp.maximum(top, jnp.max(v.reshape(ROWS // 8, 8, 512), axis=0))
-
-        old = col_m[:, cols]
-        top = lax.fori_loop(0, 2, peak, old)
-
-        def total(c, s):
-            r = pl.ds(pl.multiple_of(a * 256 + c * ROWS, ROWS), ROWS)
-            v = L[r, cols].reshape(ROWS // 8, 8, 512)
-            return s + jnp.sum(jnp.exp2(v - top[None]), axis=0)
-
-        col_s[:, cols] = lax.fori_loop(0, 2, total, col_s[:, cols] * jnp.exp2(old - top))
-        col_m[:, cols] = top
+        @pl.when(n > 0)
+        def _():
+            statistics(n - 1)
+            logits(a, b)
+
+        @pl.when(n == 0)
+        def _():
+            logits(a, b)
+
         return carry
 
     lax.fori_loop(0, len(TILES), tile, 0)
+    statistics(len(TILES) - 1)
 
     def step_of(q):
         return q + q // 2 - 2 * (q // 3)
@@ -483,8 +507,7 @@
         P8l[rows, cols] = ((g - hf) * 65536.0).astype(F8)
 
     def soften(n, carry):
-        first = STEPS[0][1]
-        p = pick(n, [first] + [m for m in range(8) if m != first])
+        p = pick(n, [m for kind, m in STEPS if kind == "t"])
         cols = pl.ds(pl.multiple_of(p * 256, 256), 256)
         cl = jnp.concatenate([cst[8, 0, pl.ds(txt_block(2 * p + j), 1), :] for j in range(2)], axis=1)
 
@@ -516,18 +539,18 @@
         return carry
 
     def loss_send(m):
-        if m == 1:
+        if m == FIRST_IMAGE:
             total = jnp.sum(acc[...]) / 1024 - 2.0 * LN2 * jnp.sum(lbuf[0])
             lbuf[0] = jnp.full((8, 128), total, F32)
             for n in range(7):
                 w.send(lbuf.at[0], ("l1", n), row_peers[n])
-        if m == 4:
+        if m == FIRST_IMAGE + 3:
             for n in range(7):
                 w.wait(("l1", n))
             lbuf[8] = sum(lbuf[n] for n in range(8))
             for n in range(3):
                 w.send(lbuf.at[8], ("l2", n), col_peers[n])
-        if m == 7:
+        if m == FIRST_IMAGE + 6:
             for n in range(3):
                 w.wait(("l2", n))
             lbuf[12] = sum(lbuf[n] for n in range(8, 12))
@@ -537,7 +560,7 @@
     def back_step(n, carry):
         is_text = pick(n, [int(kind == "t") for kind, _ in STEPS])
         arg = pick(n, [a for _, a in STEPS])
-        lax.fori_loop(pick(n, [0, 1]), pick(n, [1, 8]), soften, 0)
+        lax.fori_loop(pick(n, SOFT[:-1]), pick(n, SOFT[1:]), soften, 0)
 
         @pl.when(is_text == 1)
         def _():
@@ -551,8 +574,8 @@
 
         @pl.when(is_text == 0)
         def _():
-            r = pl.ds(pl.multiple_of(arg * 256, 256), 256)
-            r2 = pl.ds(pl.multiple_of(IMG + arg * 256, 256), 256)
+            r = pl.ds(pl.multiple_of(arg * ROWS, ROWS), ROWS)
+            r2 = pl.ds(pl.multiple_of(IMG + arg * ROWS, ROWS), ROWS)
             high = dot(Tl[r, 0:IMG], Th[0:IMG, :], 1, 0) + dot(Tl[r2, 0:IMG], Th[IMG:TXT, :], 1, 0)
             cross = dot(P8h[r, :], T8l[...], 1, 0) + dot(P8l[r, :], T8h[...], 1, 0)
             L[r, 0:E] = high + (1.0 / (65536.0 * t_scale)) * cross

time: 125 us -> 127 us (1.016)
  Pallas kernels: 119 us -> 121 us
    pallas_call x1, Pallas kernels: 119 us -> 121 us  [on_device(): pl.pallas_call(kernel, out_shape=(jax.ShapeDtypeStruct((1,), F32), jax.Sh...]
where the time goes in v5:
time: 127 us
  Pallas kernels  121 us (95%)
  between operations  3.09 us (2%)
  other arithmetic  2.43 us (2%)
    pallas_call x1, Pallas kernels, on_device(): pl.pallas_call(kernel, out_shape=(jax.ShapeDtypeStruct((1,), F32), jax.Sh...  121 us

profile of v5, /device:TPU:1, one launch (start us, length us, event | category | flops | bytes accessed | tf_op | source)
XLA Modules:
  0.0 126.9 jit_solution(7494691304509748018)
XLA Ops:
  1.3 121.4 %contrastive.1 = (f32[1]{0:T(128)}, f32[128,1280]{1,0:T(8,128)}, f32[128,1280]{1,0:T(8,128)}) custom-call(f32[1]{0:T(128)} %bitcast.2.scale_ref, f32[128,1280]{1,0:T(8,128)} %img_ref.1, f32[128,1280]{1,0:T(8,128)} %txt_ref.1), custom_call_target="tpu_custom_call" | custom-call | tf_op jit(solution)/shard_map/contrastive/pallas_call | solution.py:603
  122.7 2.4 %broadcast_multiply_fusion = (f32[128,1280]{1,0:T(8,128)}, f32[128,1280]{1,0:T(8,128)}) fusion(f32[128,1280]{1,0:T(8,128)} %get-tuple-element.8, f32[]{:T(128)} %copy.7, f32[128,1280]{1,0:T(8,128)} %get-tuple-element.7), kind=kLoop, calls=%fused_computation | loop fusion | flops 327680 | bytes 2621444 | tf_op jit(solution)/shard_map/mul | solution.py:650

commit v6 on v5

--- a/solution.py
+++ b/solution.py
@@ -135,7 +135,7 @@
     loss_ref, img_out, txt_out,
     Ib, Tb, Ih, Il, Th, Tl, L,
     P8h, P8l, I8h, I8l, T8h, T8l,
-    row_m, row_s, col_m, col_s, rst, cst, acc, lbuf,
+    row_m, row_s, col_m, col_s, rst, cst, lbuf,
     iland, tland, eye,
     send_sem, recv_sem, local_sem,
 ):
@@ -329,6 +329,24 @@
     def txt_block(s):
         return (((z + step_of(s // 4)) % 4) * 2 + (y + (s // 2) % 2) % 2) * 2 + (k + s % 2) % 2
 
+    def on_diagonal(s):
+        owner = (x * 2 + (k + s % 2) % 2) * 16 + ((z + step_of(s // 4)) % 4) * 4
+        owner = owner + (y + ((s // 2) % 2) * (4 - even)) % 4
+        bi, bt = owner // 8, owner % 8
+        here = (bi // 4 == z) & ((bi % 4) // 2 == y // 2) & (bt % 2 == k)
+        return here, step_of((bt // 2 + 4 - x) % 4) * 2 + (bi + y) % 2
+
+    def sum_diagonal(s, carry):
+        here, u = on_diagonal(s)
+
+        @pl.when(here)
+        def _():
+            r = pl.ds(pl.multiple_of(u * ROWS, ROWS), ROWS)
+            v = L[r, pl.ds(pl.multiple_of(s * ROWS, ROWS), ROWS)]
+            lbuf[0] += jnp.sum((v * eye[...]).reshape(ROWS // 8, 8, 128), axis=0)
+
+        return carry
+
     def fold_cols(s, carry):
         c = pl.ds(pl.multiple_of(s * ROWS, ROWS), ROWS)
         m8 = col_m[:, c]
@@ -386,6 +404,8 @@
         w.send(cst.at[4], ("c2", n), zs[d])
     to_eight(Ih, Il, IMG, i_scale, I8h, I8l)
     to_eight(Th, Tl, TXT, t_scale, T8h, T8l)
+    lbuf[0] = jnp.zeros((8, 128), F32)
+    lax.fori_loop(0, 16, sum_diagonal, 0)
     for n in range(7):
         w.wait(("r", n))
     m, s = merge([(rst[n, 0], rst[n, 1]) for n in range(8)])
@@ -405,7 +425,15 @@
     col_lse = m + jnp.log2(s)
     w.flush(like)
     cst[8, 0] = col_lse + 1.0
-    acc[...] = jnp.full((8, 128), LN2 * (jnp.sum(row_lse) / 8 + jnp.sum(col_lse) / 16), F32)
+    share = jnp.sum(row_lse) / 8 + jnp.sum(col_lse) / 16 - 2.0 * jnp.sum(lbuf[0])
+    lbuf[0] = jnp.full((8, 128), LN2 * share, F32)
+    for n in range(7):
+        w.open(("l1", n), lbuf, 1 + n)
+    for n in range(3):
+        w.open(("l2", n), lbuf, 9 + n)
+        w.open(("l3", n), lbuf, 13 + n)
+    for n in range(7):
+        w.send(lbuf.at[0], ("l1", n), row_peers[n])
 
     for name, land in (("I", iland), ("T", tland)):
         for p in range(2):
@@ -421,12 +449,6 @@
     for q in range(4):
         for p in range(2):
             w.open(("S", q, p), Ib, 2 * q + p)
-    for n in range(7):
-        w.open(("l1", n), lbuf, 1 + n)
-    for n in range(3):
-        w.open(("l2", n), lbuf, 9 + n)
-        w.open(("l3", n), lbuf, 13 + n)
-
     def add(dst, srcs, rows, out=None):
         step = 16
 
@@ -493,8 +515,6 @@
             add(mine.at[pl.ds(0 if d == 1 else 32, 32)], [w.wait((part, "P", d))], 32)
             w.send(mine, key, way[-d])
 
-    lbuf[0] = jnp.zeros((8, 128), F32)
-
     def put_grad(g, r, c, width):
         first, size = r
         h = g.astype(BF16)
@@ -522,35 +542,26 @@
         lax.fori_loop(0, IMG // ROWS, soft, 0)
         for j in range(2):
             s = 2 * p + j
-            owner = (x * 2 + (k + j) % 2) * 16 + ((z + step_of(s // 4)) % 4) * 4
-            owner = owner + (y + ((s // 2) % 2) * (4 - even)) % 4
-            bi, bt = owner // 8, owner % 8
-
-            @pl.when((bi // 4 == z) & ((bi % 4) // 2 == y // 2) & (bt % 2 == k))
+            here, u = on_diagonal(s)
+
+            @pl.when(here)
             def _():
-                u = step_of((bt // 2 + 4 - x) % 4) * 2 + (bi + y) % 2
                 r = pl.ds(pl.multiple_of(u * ROWS, ROWS), ROWS)
                 c = pl.ds(pl.multiple_of(s * ROWS, ROWS), ROWS)
                 v = L[r, c]
                 g = jnp.exp2(v - row_m[r, :]) + jnp.exp2(v - cl[:, 128 * j : 128 * j + 128]) - eye[...]
                 put_grad(g, (u * ROWS, ROWS), s * ROWS, ROWS)
-                lbuf[0] += jnp.sum((v * eye[...]).reshape(ROWS // 8, 8, 128), axis=0)
 
         return carry
 
     def loss_send(m):
-        if m == FIRST_IMAGE:
-            total = jnp.sum(acc[...]) / 1024 - 2.0 * LN2 * jnp.sum(lbuf[0])
-            lbuf[0] = jnp.full((8, 128), total, F32)
-            for n in range(7):
-                w.send(lbuf.at[0], ("l1", n), row_peers[n])
-        if m == FIRST_IMAGE + 3:
+        if m == 1:
             for n in range(7):
                 w.wait(("l1", n))
             lbuf[8] = sum(lbuf[n] for n in range(8))
             for n in range(3):
                 w.send(lbuf.at[8], ("l2", n), col_peers[n])
-        if m == FIRST_IMAGE + 6:
+        if m == 3:
             for n in range(3):
                 w.wait(("l2", n))
             lbuf[12] = sum(lbuf[n] for n in range(8, 12))
@@ -633,7 +644,6 @@
             vm((8, TXT), F32),
             vm((9, 2, 8, 128), F32),
             vm((9, 2, 16, 128), F32),
-            vm((8, 128), F32),
             vm((16, 8, 128), F32),
             vm((14, HALF, E), F32),
             vm((14, HALF, E), F32),

time: 127 us -> 123 us (0.969)
  Pallas kernels: 121 us -> 118 us
    pallas_call x1, Pallas kernels: 121 us -> 118 us  [on_device(): pl.pallas_call(kernel, out_shape=(jax.ShapeDtypeStruct((1,), F32), jax.Sh...]
where the time goes in v6:
time: 123 us
  Pallas kernels  118 us (96%)
  between operations  3.09 us (3%)
  other arithmetic  2.43 us (2%)
    pallas_call x1, Pallas kernels, on_device(): pl.pallas_call(kernel, out_shape=(jax.ShapeDtypeStruct((1,), F32), jax.Sh...  118 us

profile of v6, /device:TPU:1, one launch (start us, length us, event | category | flops | bytes accessed | tf_op | source)
XLA Modules:
  0.0 123.2 jit_solution(5395655812261892596)
XLA Ops:
  1.3 117.7 %contrastive.1 = (f32[1]{0:T(128)}, f32[128,1280]{1,0:T(8,128)}, f32[128,1280]{1,0:T(8,128)}) custom-call(f32[1]{0:T(128)} %bitcast.2.scale_ref, f32[128,1280]{1,0:T(8,128)} %img_ref.1, f32[128,1280]{1,0:T(8,128)} %txt_ref.1), custom_call_target="tpu_custom_call" | custom-call | tf_op jit(solution)/shard_map/contrastive/pallas_call | solution.py:614
  119.0 2.4 %broadcast_multiply_fusion = (f32[128,1280]{1,0:T(8,128)}, f32[128,1280]{1,0:T(8,128)}) fusion(f32[128,1280]{1,0:T(8,128)} %get-tuple-element.8, f32[]{:T(128)} %copy.7, f32[128,1280]{1,0:T(8,128)} %get-tuple-element.7), kind=kLoop, calls=%fused_computation | loop fusion | flops 327680 | bytes 2621444 | tf_op jit(solution)/shard_map/mul | solution.py:660

commit v7 on v6

--- a/solution.py
+++ b/solution.py
@@ -15,21 +15,24 @@
 STEP = (0, 1, 3, 2)
 F8 = jnp.float8_e4m3fn
 ROWS = 128
-HALF = ROWS // 2
+CUT = 64
+REST = ROWS - CUT
+H = REST // 2
 E = 1280
 CHUNK = 64
 IMG, TXT = 1024, 2048
 
-TILES = ((0, 0), (1, 0), (0, 2), (1, 2), (2, 0), (2, 2), (0, 1), (1, 1), (2, 1), (3, 0), (3, 1), (3, 2), (0, 3), (1, 3), (2, 3), (3, 3))
+OWN = 13
+TILES = ((0, 0), (2, 0), (0, 1), (2, 1), (1, 0), (1, 1), (0, 2), (1, 2), (2, 2), (3, 0), (3, 1), (3, 2), (0, 3), (1, 3), (2, 3), (3, 3))
 GATHER = (
-    (("TA", 0, 1), ("TB", 2, 0), ("IB", 2, 0), ("TB", 1, 0), ("IA", 0, 1), ("IB", 1, 0), ("S", 0, 0), ("TB", 0, 1),
-     ("TA", 2, 0), ("IA", 2, 0), ("TA", 1, 0), ("IB", 0, 1), ("IA", 1, 0), ("TB", 2, 1), ("TA", 2, 1),
-     ("IB", 3, 0, 0), ("TB", 3, 0, 1), ("IB", 1, 1), ("IA", 1, 1), ("TA", 1, 1), ("IA", 2, 1), ("S", 0, 1),
-     ("S", 1, 0), ("S", 2, 0), ("TB", 3, 0, 0), ("TB", 1, 1), ("IB", 3, 0, 1), ("IB", 2, 1)),
-    (("TA", 3, 0), ("IA", 3, 0), ("S", 2, 1), ("IA", 3, 1)),
-    (("TB", 3, 1),),
-    (("TA", 3, 1), ("IB", 3, 1)),
-    (("S", 1, 1),),
+    (("TA", 0, 1), ("IA", 0, 1), ("TB", 1, 0), ("IB", 2, 0), ("IA", 1, 0), ("TB", 2, 0), ("S", 0, 0), ("TB", 0, 1),
+     ("IB", 0, 1), ("TA", 1, 0), ("IA", 2, 0), ("IB", 1, 0), ("TA", 2, 0), ("TB", 1, 1), ("IB", 2, 1),
+     ("TA", 1, 1), ("IA", 2, 1), ("IA", 1, 1), ("TA", 2, 1), ("S", 0, 1), ("S", 1, 0), ("S", 2, 0),
+     ("TB", 3, 0, 1), ("IB", 3, 0, 1), ("IB", 1, 1), ("TB", 3, 0, 0), ("TB", 2, 1), ("IB", 3, 0, 0)),
+    (("S", 1, 1), ("TA", 3, 0), ("IA", 3, 1), ("TA", 3, 1), ("IA", 3, 0)),
+    (),
+    (("IB", 3, 1), ("TB", 3, 1)),
+    (("S", 2, 1),),
     (),
     (("S", 3, 0),),
     (),
@@ -44,25 +47,24 @@
     (),
 )
 
-STEPS = (("t", 7), ("t", 6), ("i", 7), ("t", 5), ("i", 5), ("t", 3), ("t", 4), ("i", 6), ("i", 3), ("t", 1), ("t", 2), ("i", 2), ("i", 1), ("i", 4), ("t", 0), ("i", 0))
+STEPS = (("t", 7), ("t", 6), ("i", 7), ("t", 3), ("i", 6), ("i", 5), ("t", 2), ("t", 5), ("t", 1), ("i", 3), ("t", 4), ("i", 2), ("i", 1), ("i", 4), ("t", 0), ("i", 0))
 RETURN = (
     (("S", 3, 1),),
     (("S", 3, 0),),
-    (("TB", "Y", 3), ("IB", "Y", 3), ("TA", "P", 1), ("IA", "P", 1), ("TA", "P", 0)),
-    (("S", 2, 1),),
-    (("IA", "D", 1, 1),),
-    (("S", 1, 1), ("TB", "Y", 2), ("IB", "Y", 2)),
-    (("S", 2, 0), ("TA", "D", 1, 1)),
-    (("IB", "P", -1), ("TA", "D", 1, -1), ("IA", "P", 0)),
-    (),
-    (("S", 0, 1), ("IA", "D", 1, -1), ("TB", "Y", 1), ("TA", "D", 0, 1), ("IB", "Y", 1)),
-    (("S", 1, 0), ("TB", "P", -1)),
-    (("IB", "P", 1),),
-    (("IA", "D", 0, -1), ("TA", "2"), ("TA", "D", 0, -1), ("IB", "Y", 0)),
-    (("IA", "D", 0, 1), ("TB", "P", 1)),
-    (("S", 0, 0),),
-    (("IB", "D", -1), ("TB", "D", -1), ("IA", "2"), ("TB", "Y", 0), ("TB", "D", 1), ("IB", "D", 1), ("T", "F"),
-     ("I", "F")),
+    (("TA", "P", 0), ("TA", "P", 1), ("TB", "Y", 3), ("IA", "P", 1), ("IB", "Y", 3)),
+    (("S", 1, 1),),
+    (("IA", "P", 0),),
+    (("TB", "Y", 1), ("IB", "Y", 2)),
+    (("S", 1, 0), ("IA", "D", 1, 1)),
+    (("S", 2, 1), ("IB", "P", -1), ("TA", "D", 1, -1), ("TB", "P", 1)),
+    (("S", 0, 1),),
+    (("IB", "Y", 1), ("IA", "D", 1, -1), ("TB", "Y", 2), ("TB", "P", -1), ("TA", "D", 1, 1), ("IB", "P", 1)),
+    (("S", 2, 0),),
+    (("TA", "D", 0, -1), ("TB", "Y", 0), ("IA", "D", 0, -1)),
+    (("TA", "D", 0, 1), ("IB", "Y", 0)),
+    (("IA", "D", 0, 1),),
+    (("TB", "D", -1), ("S", 0, 0)),
+    (("TB", "D", 1), ("IB", "D", -1), ("TA", "2"), ("IB", "D", 1), ("IA", "2"), ("T", "F"), ("I", "F")),
 )
 
 
@@ -136,7 +138,7 @@
     Ib, Tb, Ih, Il, Th, Tl, L,
     P8h, P8l, I8h, I8l, T8h, T8l,
     row_m, row_s, col_m, col_s, rst, cst, lbuf,
-    iland, tland, eye,
+    ialand, ibland, taland, tbland, eye,
     send_sem, recv_sem, local_sem,
 ):
     i, t = lax.axis_index("img"), lax.axis_index("txt")
@@ -166,7 +168,7 @@
             return Ib.at[0, pl.ds(0, shape[0])]
         return {2: lbuf, 3: rst if shape[-2] == 8 else cst}[len(shape)].at[0]
 
-    lo, hi = pl.ds(0, HALF), pl.ds(HALF, HALF)
+    lo, hi = pl.ds(0, CUT), pl.ds(CUT, REST)
     ring = {"I": xs, "T": zs}
     across = {"I": yi, "T": yt}
     own = {"I": img_ref, "T": txt_ref}
@@ -182,7 +184,7 @@
                 w.open((name + "A", q, p), *place(name, q, p), lo)
                 if (q, p) == (3, 0):
                     for n in range(2):
-                        w.open((name + "B", 3, 0, n), *place(name, 3, 0), pl.ds(HALF + 32 * n, 32))
+                        w.open((name + "B", 3, 0, n), *place(name, 3, 0), pl.ds(CUT + H * n, H))
                 else:
                     w.open((name + "B", q, p), *place(name, q, p), hi)
     for q in range(4):
@@ -212,7 +214,7 @@
             source, dst = (q, 0), across[name]
         elif len(key) == 4:
             source, dst = (2 - key[3], 0), ring[name][1 - 2 * key[3]]
-            rows = pl.ds(HALF + 32 * key[3], 32)
+            rows = pl.ds(CUT + H * key[3], H)
         elif q == 3:
             source, dst = (2 - p, p), ring[name][1 - 2 * p]
         else:
@@ -222,7 +224,7 @@
 
     own_t = pltpu.make_async_copy(txt_ref, Tb.at[0], local_sem.at[0])
     own_i = pltpu.make_async_copy(img_ref, Ib.at[0], local_sem.at[1])
-    for key in GATHER[0][:13]:
+    for key in GATHER[0][:OWN]:
         gather_send(key)
     own_t.start()
     own_i.start()
@@ -249,13 +251,29 @@
 
     own_i.wait()
     own_t.wait()
-    for key in GATHER[0][13:]:
+    done = set()
+
+    def split_arrived():
+        for q in range(4):
+            for p in range(2):
+                if not any(key in w.arrivals for key in keys_of("I", q, p)) and ("I", q, p) not in done:
+                    done.add(("I", q, p))
+                    split_rows(Ib, 2 * q + p, 1, Ih, Il)
+                if not any(key in w.arrivals for key in keys_of("T", q, p)) and ("T", q, p) not in done:
+                    done.add(("T", q, p))
+                    split_rows(Tb, 4 * q + 2 * p, 1, Th, Tl)
+                if ("S", q, p) not in w.arrivals and ("S", q, p) not in done:
+                    done.add(("S", q, p))
+                    split_rows(Tb, 4 * q + 2 * p + 1, 1, Th, Tl)
+
+    for n, key in enumerate(GATHER[0][OWN:]):
         gather_send(key)
+        if n == 5:
+            w.need(("S", 0, 0))
+            split_arrived()
+    split_arrived()
 
     s2 = scale_ref[0] * LOG2E
-    seen_i = [int(qi not in [a for a, _ in TILES[:n]]) for n, (qi, _) in enumerate(TILES)]
-    seen_t = [int(qt not in [b for _, b in TILES[:n]]) for n, (_, qt) in enumerate(TILES)]
-
     def tile_at(n):
         return pick(n, [qi for qi, _ in TILES]), pick(n, [qt for _, qt in TILES])
 
@@ -295,16 +313,9 @@
                         gather_send(key)
                 for p in range(2):
                     w.need(*keys_of("I", qi, p), *keys_of("T", qt, p), ("S", qt, p))
+                split_arrived()
 
         a, b = tile_at(n)
-
-        @pl.when(pick(n, seen_i) == 1)
-        def _():
-            split_rows(Ib, 2 * a, 2, Ih, Il)
-
-        @pl.when(pick(n, seen_t) == 1)
-        def _():
-            split_rows(Tb, 4 * b, 4, Th, Tl)
 
         @pl.when(n > 0)
         def _():
@@ -435,22 +446,22 @@
     for n in range(7):
         w.send(lbuf.at[0], ("l1", n), row_peers[n])
 
-    for name, land in (("I", iland), ("T", tland)):
+    for name, land_a, land_b in (("I", ialand, ibland), ("T", taland, tbland)):
         for p in range(2):
-            w.open((name + "A", "P", p), land, p)
+            w.open((name + "A", "P", p), land_a, p)
             for n, d in enumerate((1, -1)):
-                w.open((name + "A", "D", p, d), land, 2 + 2 * p + n)
-        w.open((name + "A", "2"), land, 6)
+                w.open((name + "A", "D", p, d), land_a, 2 + 2 * p + n)
+        w.open((name + "A", "2"), land_a, 6)
         for q in range(4):
-            w.open((name + "B", "Y", q), land, 7 + q)
+            w.open((name + "B", "Y", q), land_b, q)
         for n, d in enumerate((1, -1)):
-            w.open((name + "B", "P", d), land, 11, pl.ds(32 * n, 32))
-            w.open((name + "B", "D", d), land, 12 + n)
+            w.open((name + "B", "P", d), land_b, 4, pl.ds(H * n, H))
+            w.open((name + "B", "D", d), land_b, 5 + n)
     for q in range(4):
         for p in range(2):
             w.open(("S", q, p), Ib, 2 * q + p)
     def add(dst, srcs, rows, out=None):
-        step = 16
+        step = 16 if rows % 16 == 0 else 8
 
         def body(b, carry):
             r = pl.ds(pl.multiple_of(b * step, step), step)
@@ -483,36 +494,36 @@
             out = img_out if name == "I" else txt_out
             A, B = name + "A", name + "B"
             srcs = [w.wait((A, "D", 0, 1)), w.wait((A, "D", 0, -1)), w.wait((A, "2"))]
-            add(sums(name, 0, 0, 0, HALF), srcs, HALF, out.at[lo])
+            add(sums(name, 0, 0, 0, CUT), srcs, CUT, out.at[lo])
             srcs = [w.wait((B, "Y", 0)), w.wait((B, "D", 1)), w.wait((B, "D", -1))]
-            add(sums(name, 0, 0, HALF, HALF), srcs, HALF, out.at[hi])
+            add(sums(name, 0, 0, CUT, REST), srcs, REST, out.at[hi])
         elif part[1] == "A":
             if kind == "P":
-                w.send(sums(name, 3, key[2], 0, HALF), key, way[2 * key[2] - 1])
+                w.send(sums(name, 3, key[2], 0, CUT), key, way[2 * key[2] - 1])
             elif kind == "D":
                 p, d = key[2:]
-                mine = sums(name, 2 if d == 1 else 1, p, 0, HALF)
+                mine = sums(name, 2 if d == 1 else 1, p, 0, CUT)
                 if p == (1 - d) // 2:
-                    add(mine, [w.wait((part, "P", p))], HALF)
+                    add(mine, [w.wait((part, "P", p))], CUT)
                 w.send(mine, key, way[-d])
             else:
-                mine = sums(name, 0, 1, 0, HALF)
-                add(mine, [w.wait((part, "D", 1, 1)), w.wait((part, "D", 1, -1))], HALF)
+                mine = sums(name, 0, 1, 0, CUT)
+                add(mine, [w.wait((part, "D", 1, 1)), w.wait((part, "D", 1, -1))], CUT)
                 w.send(mine, key, across[name])
         elif kind == "Y":
-            w.send(sums(name, key[2], 1, HALF, HALF), key, across[name])
+            w.send(sums(name, key[2], 1, CUT, REST), key, across[name])
         elif kind == "P":
             d = key[2]
             if (name, "far") not in summed:
                 summed.add((name, "far"))
-                add(sums(name, 3, 0, HALF, HALF), [w.wait((part, "Y", 3))], HALF)
-            w.send(sums(name, 3, 0, HALF if d == 1 else HALF + 32, 32), key, way[-d])
+                add(sums(name, 3, 0, CUT, REST), [w.wait((part, "Y", 3))], REST)
+            w.send(sums(name, 3, 0, CUT if d == 1 else CUT + H, H), key, way[-d])
         else:
             d = key[2]
             q = 2 if d == 1 else 1
-            mine = sums(name, q, 0, HALF, HALF)
-            add(mine, [w.wait((part, "Y", q))], HALF)
-            add(mine.at[pl.ds(0 if d == 1 else 32, 32)], [w.wait((part, "P", d))], 32)
+            mine = sums(name, q, 0, CUT, REST)
+            add(mine, [w.wait((part, "Y", q))], REST)
+            add(mine.at[pl.ds(0 if d == 1 else H, H)], [w.wait((part, "P", d))], H)
             w.send(mine, key, way[-d])
 
     def put_grad(g, r, c, width):
@@ -645,8 +656,10 @@
             vm((9, 2, 8, 128), F32),
             vm((9, 2, 16, 128), F32),
             vm((16, 8, 128), F32),
-            vm((14, HALF, E), F32),
-            vm((14, HALF, E), F32),
+            vm((7, CUT, E), F32),
+            vm((7, REST, E), F32),
+            vm((7, CUT, E), F32),
+            vm((7, REST, E), F32),
             vm((ROWS, ROWS), F32),
             pltpu.SemaphoreType.DMA((56,)),
             pltpu.SemaphoreType.DMA((112,)),

time: 123 us -> 122 us (level)
  no operation moved by 1% of the time
where the time goes in v7:
time: 122 us
  Pallas kernels  117 us (96%)
  between operations  3.09 us (3%)
  other arithmetic  2.43 us (2%)
    pallas_call x1, Pallas kernels, on_device(): pl.pallas_call(kernel, out_shape=(jax.ShapeDtypeStruct((1,), F32), jax.Sh...  117 us

profile of v7, /device:TPU:1, one launch (start us, length us, event | category | flops | bytes accessed | tf_op | source)
XLA Modules:
  0.0 122.2 jit_solution(1454569292928686690)
XLA Ops:
  1.3 116.7 %contrastive.1 = (f32[1]{0:T(128)}, f32[128,1280]{1,0:T(8,128)}, f32[128,1280]{1,0:T(8,128)}) custom-call(f32[1]{0:T(128)} %bitcast.2.scale_ref, f32[128,1280]{1,0:T(8,128)} %img_ref.1, f32[128,1280]{1,0:T(8,128)} %txt_ref.1), custom_call_target="tpu_custom_call" | custom-call | tf_op jit(solution)/shard_map/contrastive/pallas_call | solution.py:625
  118.0 2.4 %broadcast_multiply_fusion = (f32[128,1280]{1,0:T(8,128)}, f32[128,1280]{1,0:T(8,128)}) fusion(f32[128,1280]{1,0:T(8,128)} %get-tuple-element.8, f32[]{:T(128)} %copy.7, f32[128,1280]{1,0:T(8,128)} %get-tuple-element.7), kind=kLoop, calls=%fused_computation | loop fusion | flops 327680 | bytes 2621444 | tf_op jit(solution)/shard_map/mul | solution.py:673

commit v8 on v7

--- a/solution.py
+++ b/solution.py
@@ -138,7 +138,7 @@
     Ib, Tb, Ih, Il, Th, Tl, L,
     P8h, P8l, I8h, I8l, T8h, T8l,
     row_m, row_s, col_m, col_s, rst, cst, lbuf,
-    ialand, ibland, taland, tbland, eye,
+    ialand, ibland, taland, tbland, eye, span,
     send_sem, recv_sem, local_sem,
 ):
     i, t = lax.axis_index("img"), lax.axis_index("txt")
@@ -231,6 +231,7 @@
 
     rows_iota = lax.broadcasted_iota(jnp.int32, (ROWS, ROWS), 0)
     cols_iota = lax.broadcasted_iota(jnp.int32, (ROWS, ROWS), 1)
+    span[...] = jnp.zeros((2, 8, E), F32)
     eye[...] = (rows_iota == cols_iota).astype(F32)
     row_m[...] = jnp.full((IMG, 128), -jnp.inf, F32)
     row_s[...] = jnp.zeros((IMG, 128), F32)
@@ -242,6 +243,8 @@
             n = first + b // 4
             o = pl.ds(pl.multiple_of(first * ROWS + b * 32, 32), 32)
             v = src[n, pl.ds(pl.multiple_of((b % 4) * 32, 32), 32), :]
+            at = 0 if high is Ih else 1
+            span[at] = jnp.maximum(span[at], jnp.max(jnp.abs(v).reshape(4, 8, E), axis=0))
             h = v.astype(BF16)
             high[o, :] = h
             low[o, :] = (v - h.astype(F32)).astype(BF16)
@@ -389,15 +392,8 @@
     lax.fori_loop(0, 8, fold_rows, 0)
     for n in range(7):
         w.send(rst.at[0], ("r", n), row_peers[n])
-    def largest(src, count):
-        def body(b, top):
-            v = jnp.abs(src[pl.ds(pl.multiple_of(b * 64, 64), 64), :]).astype(F32)
-            return jnp.maximum(top, jnp.max(v.reshape(8, 8, E), axis=0))
-
-        return jnp.max(lax.fori_loop(0, count // 64, body, jnp.zeros((8, E), F32)))
-
-    i_scale = 240.0 / jnp.maximum(largest(Ih, IMG), 1e-30)
-    t_scale = 240.0 / jnp.maximum(largest(Th, TXT), 1e-30)
+    i_scale = 240.0 / jnp.maximum(jnp.max(span[0]), 1e-30)
+    t_scale = 240.0 / jnp.maximum(jnp.max(span[1]), 1e-30)
 
     def to_eight(high, low, count, scale, high8, low8):
         def body(b, carry):
@@ -661,6 +657,7 @@
             vm((7, CUT, E), F32),
             vm((7, REST, E), F32),
             vm((ROWS, ROWS), F32),
+            vm((2, 8, E), F32),
             pltpu.SemaphoreType.DMA((56,)),
             pltpu.SemaphoreType.DMA((112,)),
             pltpu.SemaphoreType.DMA((2,)),

time: 122 us -> 123 us (level)
  no operation moved by 1% of the time
where the time goes in v8:
time: 123 us; the launch traced here: 122 us
  Pallas kernels  117 us (95%)
  between operations  3.09 us (3%)
  other arithmetic  2.43 us (2%)
    pallas_call x1, Pallas kernels, on_device(): pl.pallas_call(kernel, out_shape=(jax.ShapeDtypeStruct((1,), F32), jax.Sh...  117 us

profile of v8, /device:TPU:1, one launch (start us, length us, event | category | flops | bytes accessed | tf_op | source)
XLA Modules:
  0.0 122.4 jit_solution(7975664318390028866)
XLA Ops:
  1.3 116.9 %contrastive.1 = (f32[1]{0:T(128)}, f32[128,1280]{1,0:T(8,128)}, f32[128,1280]{1,0:T(8,128)}) custom-call(f32[1]{0:T(128)} %bitcast.2.scale_ref, f32[128,1280]{1,0:T(8,128)} %img_ref.1, f32[128,1280]{1,0:T(8,128)} %txt_ref.1), custom_call_target="tpu_custom_call" | custom-call | tf_op jit(solution)/shard_map/contrastive/pallas_call | solution.py:621
  118.2 2.4 %broadcast_multiply_fusion = (f32[128,1280]{1,0:T(8,128)}, f32[128,1280]{1,0:T(8,128)}) fusion(f32[128,1280]{1,0:T(8,128)} %get-tuple-element.8, f32[]{:T(128)} %copy.7, f32[128,1280]{1,0:T(8,128)} %get-tuple-element.7), kind=kLoop, calls=%fused_computation | loop fusion | flops 327680 | bytes 2621444 | tf_op jit(solution)/shard_map/mul | solution.py:670
